TPU v7x, 512 devices: a whole 4x4x16 slice. The times are simulated.
512 devices in a mesh: row: 16 (over z_lo, core), col: 8 (over z_hi, x), feat: 4 (over y).
Axes of the slice: x: 4, y: 4, z: 16 (z_hi: 2, z_lo: 8; z = z_hi * 8 + z_lo), core: 2. Of those that a mesh axis runs over, the one named last changes fastest.
Arguments:
- snapshots: bfloat16 [2048, 32768], P(('row', 'col'), 'feat'), may hold values from -6 to 6
- start_block: float32 [2048, 32], P('row'), may hold values from -6 to 6
Outputs:
- eigen_basis: float32 [2048, 32], P('row')
All inputs are finite; a program needn't handle non-finite values.
Results may differ from a plain program's by a relative error of at most 0.0003.
Values may be sent and summed in bfloat16 or wider, within the bound.
A program may use at most 64 MiB of HBM per device.

v0:
```python
import math

import jax
import jax.numpy as jnp
from jax import lax
from jax.sharding import PartitionSpec as P

PTS = 32768
LAGS = 128
ITERS = 6


kernel_spread = 0.25
highest = lax.Precision.HIGHEST


def copy_for_each(x, axis):
    copies = jnp.broadcast_to(x, (lax.axis_size(axis), *x.shape))
    return lax.all_to_all(copies, axis, split_axis=0, concat_axis=0, tiled=True)


def taken_together(x, axis):
    everything = copy_for_each(x, axis)
    return jnp.sum(everything, axis=0)


def shifted(x, axis, by):
    length = lax.axis_size(axis)
    pairs = [(i, i + by) for i in range(length) if 0 <= i + by < length]
    return lax.ppermute(x, axis, pairs)


def joined_along(tiles, dim):
    dims = list(tiles.shape[1:])
    dims[dim] *= tiles.shape[0]
    return jnp.moveaxis(tiles, 0, dim).reshape(dims)


def collect(x, axis, dim):
    return joined_along(copy_for_each(x, axis), dim)


def gathered_total(x, axis):
    tiles = lax.all_gather(x, axis)
    return tiles.sum(axis=0)


def diagonal_window(extended, lag_count):
    running = None
    offset = 0
    partial_sum = extended
    levels = lag_count.bit_length()
    for level in range(levels):
        stride = 1 << level
        if lag_count & stride:
            running = partial_sum
            offset = offset + stride
        if level + 1 < levels:
            partial_sum = partial_sum[:-stride, :-stride] + partial_sum[stride:, stride:]
    return running


def orthonormal(product, gram_sum):
    factor = jnp.linalg.cholesky(gram_sum)
    return jax.scipy.linalg.solve_triangular(factor, product.T, lower=True).T


def square_norms(fields):
    widened = fields.astype(jnp.float32)
    return jnp.sum(widened * widened, axis=1)


def body(snapshots, start_block):
    row_total = lax.axis_size("row")
    col_total = lax.axis_size("col")
    row_place = lax.axis_index("row")
    col_place = lax.axis_index("col")
    shard_rows = snapshots.shape[0]
    block_rows = shard_rows * col_total
    pairing = row_total // col_total
    block_cols = block_rows * pairing
    own_rows = lax.all_gather(snapshots, "col", axis=0, tiled=True)
    own_norms = square_norms(own_rows)
    piece = lax.all_gather(snapshots, "row", axis=0, tiled=True)
    piece_norms = square_norms(piece)
    products = lax.dot_general(
        own_rows, piece, (((1,), (1,)), ((), ())), preferred_element_type=jnp.float32
    )
    partial_dist = own_norms[:, None] + piece_norms[None, :] - 2.0 * products
    distance = taken_together(partial_dist, "feat")
    grouped = distance.reshape(block_rows, col_total, pairing, shard_rows)
    moved = lax.all_to_all(grouped, "col", split_axis=1, concat_axis=1, tiled=True)
    distance = moved.transpose(0, 2, 1, 3).reshape(block_rows, block_cols)
    rim_width = LAGS - 1
    top_rim = shifted(distance[block_rows - rim_width :], "row", 1)
    upper = jnp.concatenate([top_rim, distance], axis=0)
    left_side = shifted(upper[:, block_cols - rim_width :], "col", 1)
    extended = jnp.concatenate([left_side, upper], axis=1)
    lagged = diagonal_window(extended, LAGS)
    row_ids = row_place * block_rows + lax.broadcasted_iota(jnp.int32, (block_rows, block_cols), 0)
    col_ids = col_place * block_cols + lax.broadcasted_iota(jnp.int32, (block_rows, block_cols), 1)
    counts = jnp.minimum(jnp.minimum(row_ids, col_ids), rim_width) + 1
    kernel = jnp.exp(-(lagged / (counts.astype(jnp.float32) * PTS)) / kernel_spread)
    row_degree = taken_together(jnp.sum(kernel, axis=1), "col")
    every_degree = collect(row_degree, "row", 0)
    col_degree = lax.dynamic_slice_in_dim(every_degree, col_place * block_cols, block_cols)
    markov = kernel * lax.rsqrt(row_degree)[:, None] * lax.rsqrt(col_degree)[None, :]
    basis = start_block
    for rounds in range(ITERS // 2):
        product = lax.dot_general(
            markov,
            basis,
            (((0,), (0,)), ((), ())),
            precision=highest,
            preferred_element_type=jnp.float32,
        )
        summed_cols = gathered_total(product, "row")
        row_product = jnp.dot(
            markov, summed_cols, precision=highest, preferred_element_type=jnp.float32
        )
        summed_rows = taken_together(row_product, "col")
        local_gram = jnp.dot(
            summed_rows.T, summed_rows, precision=highest, preferred_element_type=jnp.float32
        )
        gram_rows = taken_together(local_gram, "row")
        basis = orthonormal(summed_rows, gram_rows)
    return basis * math.sqrt(row_total * block_rows)


def solution(mesh):
    placed = (P(("row", "col"), "feat"), P("row", None))
    return jax.shard_map(
        body, mesh=mesh, in_specs=placed, out_specs=P("row", None), check_vma=False
    )
```

profile of v0, /device:TPU:1, one launch (start us, length us, event | category | flops | bytes accessed | tf_op | source)
XLA Modules:
  0.0 553.9 jit_solution(12757546459671542921)
XLA Ops:
  8.0 124.7 %all-gather.6.cloned.1.call-done = bf16[128,8192]{1,0:T(8,128)(2,1)} async-done(((bf16[16,8192]{1,0:T(8,128)(2,1)}), bf16[128,8192]{1,0:T(8,128)(2,1)}) %all-gather.6.cloned.1.call-update) | async-done | bytes 2097168 | tf_op jit(solution)/shard_map/all_gather | solution.py:82
  132.7 2.2 multiply_reduce_fusion.1
  134.9 99.4 %all-gather.8.cloned.1.call-done = bf16[256,8192]{1,0:T(8,128)(2,1)} async-done(((bf16[16,8192]{1,0:T(8,128)(2,1)}), bf16[256,8192]{1,0:T(8,128)(2,1)}) %all-gather.8.cloned.1.call-update) | async-done | bytes 4194320 | tf_op jit(solution)/shard_map/all_gather | solution.py:84
  234.3 3.3 multiply_reduce_fusion
  237.7 1.5 fusion
  239.3 9.5 %all_to_all.52 = f32[4,128,256]{2,1,0:T(8,128)S(1)} all-to-all(f32[4,128,256]{2,1,0:T(8,128)S(1)} %broadcast_in_dim.32), channel_id=1, replica_groups=mesh['row'=16,'col'=8,'feat'=4] {'feat'}, dimensions={0} | all-to-all | bytes 1048576 | tf_op jit(solution)/shard_map/all_to_all | solution.py:19
  248.9 22.6 %all_to_all.53 = f32[128,8,2,16]{0,3,2,1:T(8,128)S(1)} all-to-all(f32[128,8,2,16]{0,3,2,1:T(8,128)S(1)} %bitcast.80), channel_id=1, replica_groups=mesh['row'=16,'col'=8,'feat'=4] {'col'}, dimensions={1} | all-to-all | bytes 262144 | tf_op jit(solution)/shard_map/all_to_all | solution.py:92
  271.6 3.8 collective-permute-start
  275.4 8.3 %collective-permute-done = f32[127,256]{0,1:T(8,128)S(1)} collective-permute-done((f32[127,256]{0,1:T(8,128)S(1)}, f32[127,256]{0,1:T(8,128)S(1)}, u32[]{:S(2)}, u32[]{:S(2)}) %collective-permute-start) | collective-permute-done | bytes 130080 | tf_op jit(solution)/shard_map/ppermute | solution.py:30
  283.8 1.6 collective-permute-start.1
  285.4 2.7 collective-permute-done.1
  289.4 27.5 %all_to_all.54 = f32[8,1,128]{2,1,0:T(1,128)S(1)} all-to-all(f32[8,1,128]{2,1,0:T(1,128)S(1)} %broadcast_in_dim.33), channel_id=1, replica_groups=mesh['row'=16,'col'=8,'feat'=4] {'col'}, dimensions={0} | all-to-all | bytes 8192 | tf_op jit(solution)/shard_map/all_to_all | solution.py:19
  317.6 7.7 %all-to-all-start.3 = ((f32[16,1,128]{2,1,0:T(1,128)}), f32[16,1,128]{2,1,0:T(1,128)S(1)}, u32[]{:S(2)}, u32[]{:S(2)}) async-start(f32[16,1,128]{2,1,0:T(1,128)} %broadcast_in_dim.34), calls=%async_computation.3 | async-start | bytes 16384 | tf_op jit(solution)/shard_map/all_to_all | solution.py:19
  325.3 9.6 %all-to-all-done.3 = f32[16,1,128]{2,1,0:T(1,128)S(1)} async-done(((f32[16,1,128]{2,1,0:T(1,128)}), f32[16,1,128]{2,1,0:T(1,128)S(1)}, u32[]{:S(2)}, u32[]{:S(2)}) %all-to-all-start.3) | async-done | bytes 8224 | tf_op jit(solution)/shard_map/all_to_all | solution.py:19
  335.3 28.5 %all-gather = f32[4096,32]{0,1:T(8,128)S(1)} all-gather(f32[256,32]{0,1:T(8,128)S(1)} %fusion.29), channel_id=2, replica_groups=mesh['row'=16,'col'=8,'feat'=4] {'row'}, dimensions={0}, use_global_device_ids=true | all-gather | bytes 557056 | tf_op jit(solution)/shard_map/all_gather | solution.py:44
  364.4 16.5 %all_to_all.55 = f32[8,128,32]{1,2,0:T(8,128)S(1)} all-to-all(f32[8,128,32]{1,2,0:T(8,128)S(1)} %broadcast_in_dim.35), channel_id=1, replica_groups=mesh['row'=16,'col'=8,'feat'=4] {'col'}, dimensions={0} | all-to-all | bytes 262144 | tf_op jit(solution)/shard_map/all_to_all | solution.py:19
  381.3 14.9 %all_to_all.56 = f32[16,1,1024]{2,1,0:T(1,128)S(1)} all-to-all(f32[16,1,1024]{2,1,0:T(1,128)S(1)} %reshape.39), channel_id=1, replica_groups=mesh['row'=16,'col'=8,'feat'=4] {'row'}, dimensions={0} | all-to-all | bytes 131072 | tf_op jit(solution)/shard_map/all_to_all | solution.py:19
  397.7 2.9 cholesky.59
  402.1 2.4 custom-call.7
  405.1 29.9 %all-gather.1 = f32[4096,32]{0,1:T(8,128)S(1)} all-gather(f32[256,32]{0,1:T(8,128)S(1)} %fusion.27), channel_id=3, replica_groups=mesh['row'=16,'col'=8,'feat'=4] {'row'}, dimensions={0}, use_global_device_ids=true | all-gather | bytes 557056 | tf_op jit(solution)/shard_map/all_gather | solution.py:44
  435.6 16.5 %all_to_all.57 = f32[8,128,32]{1,2,0:T(8,128)S(1)} all-to-all(f32[8,128,32]{1,2,0:T(8,128)S(1)} %broadcast_in_dim.37), channel_id=1, replica_groups=mesh['row'=16,'col'=8,'feat'=4] {'col'}, dimensions={0} | all-to-all | bytes 262144 | tf_op jit(solution)/shard_map/all_to_all | solution.py:19
  452.5 13.9 %all_to_all.58 = f32[16,1,1024]{2,1,0:T(1,128)S(1)} all-to-all(f32[16,1,1024]{2,1,0:T(1,128)S(1)} %reshape.41), channel_id=1, replica_groups=mesh['row'=16,'col'=8,'feat'=4] {'row'}, dimensions={0} | all-to-all | bytes 131072 | tf_op jit(solution)/shard_map/all_to_all | solution.py:19
  466.5 0.8 reduce.6
  467.5 2.9 cholesky.70
  471.9 2.4 custom-call.8
  474.9 29.7 %all-gather.2 = f32[4096,32]{0,1:T(8,128)S(1)} all-gather(f32[256,32]{0,1:T(8,128)S(1)} %fusion.25), channel_id=4, replica_groups=mesh['row'=16,'col'=8,'feat'=4] {'row'}, dimensions={0}, use_global_device_ids=true | all-gather | bytes 557056 | tf_op jit(solution)/shard_map/all_gather | solution.py:44
  505.2 18.8 %all_to_all.59 = f32[8,128,32]{1,2,0:T(8,128)S(1)} all-to-all(f32[8,128,32]{1,2,0:T(8,128)S(1)} %broadcast_in_dim.39), channel_id=1, replica_groups=mesh['row'=16,'col'=8,'feat'=4] {'col'}, dimensions={0} | all-to-all | bytes 262144 | tf_op jit(solution)/shard_map/all_to_all | solution.py:19
  524.3 14.1 %all_to_all.60 = f32[16,1,1024]{2,1,0:T(1,128)S(1)} all-to-all(f32[16,1,1024]{2,1,0:T(1,128)S(1)} %reshape.43), channel_id=1, replica_groups=mesh['row'=16,'col'=8,'feat'=4] {'row'}, dimensions={0} | all-to-all | bytes 131072 | tf_op jit(solution)/shard_map/all_to_all | solution.py:19
  538.4 0.8 reduce.7
  539.5 2.9 cholesky.81
  543.7 2.4 custom-call.9
  546.2 0.8 fusion.1
  (84 shorter events, 14.2 us)
Async XLA Ops:
  6.5 328.5 %copy-start = (f32[128,32]{0,1:T(8,128)S(1)}, f32[128,32]{0,1:T(8,128)}, u32[]{:S(2)}) copy-start(f32[128,32]{0,1:T(8,128)} %param.6) | copy-start | bytes 49156
  6.5 126.1 %all-gather.6.cloned.1.call-start = ((), (), s32[]{:S(2)}) async-start(), calls=%async_computation.10 | async-start | bytes 2359296 | tf_op jit(solution)/shard_map/all_gather | solution.py:82
  7.3 227.0 %all-gather.8.cloned.1.call-start = ((), (), s32[]{:S(2)}) async-start(), calls=%async_computation.11 | async-start | bytes 4456448 | tf_op jit(solution)/shard_map/all_gather | solution.py:84
  132.7 104.9 %copy-start.2 = (bf16[128,8192]{1,0:T(8,128)(2,1)S(1)}, bf16[128,8192]{1,0:T(8,128)(2,1)}, u32[]{:S(2)}) copy-start(bf16[128,8192]{1,0:T(8,128)(2,1)} %all-gather.6.cloned.1.call-done) | copy-start | bytes 6291460
  234.3 3.4 copy-start.1
  271.6 12.1 %collective-permute-start = (f32[127,256]{0,1:T(8,128)S(1)}, f32[127,256]{0,1:T(8,128)S(1)}, u32[]{:S(2)}, u32[]{:S(2)}) collective-permute-start(f32[127,256]{0,1:T(8,128)S(1)} %bitcast.81), channel_id=1, source_target_pairs={{0,32},{32,64},{64,96},{96,128},{128,160},{160,192},{192,224},{224... | collective-permute-start | bytes 390152 | tf_op jit(solution)/shard_map/ppermute | solution.py:30
  283.8 4.3 collective-permute-start.1
  317.6 17.3 %all-to-all-start.3 = ((f32[16,1,128]{2,1,0:T(1,128)}), f32[16,1,128]{2,1,0:T(1,128)S(1)}, u32[]{:S(2)}, u32[]{:S(2)}) async-start(f32[16,1,128]{2,1,0:T(1,128)} %broadcast_in_dim.34), calls=%async_computation.3 | async-start | bytes 16384 | tf_op jit(solution)/shard_map/all_to_all | solution.py:19
Sparse Core Ops, SparseCore 0:
  10.6 122.0 all-gather.5
  134.7 99.4 all-gather.7
where the time goes:
time: 554 us
  waiting for transfers between devices  246 us (44%)
  blocking collectives  243 us (44%)
  other arithmetic  30 us (5%)
  between operations  13.8 us (2%)
  starting transfers between devices  13.1 us (2%)
    all_to_all x8, blocking collectives, copy_for_each(): return lax.all_to_all(copies, axis, split_axis=0, concat_axis=0, tiled=True)  132 us
    all_gather x1, waiting for transfers between devices, body(): own_rows = lax.all_gather(snapshots, 'col', axis=0, tiled=True)  125 us
    all_gather x1, waiting for transfers between devices, body(): piece = lax.all_gather(snapshots, 'row', axis=0, tiled=True)  99.4 us
    all_gather x3, blocking collectives, gathered_total(): tiles = lax.all_gather(x, axis)  88.2 us
    all_to_all x1, blocking collectives, body(): lax.all_to_all(grouped, 'col', split_axis=1, concat_axis=1, tiled=True)  22.6 us
  transfers between devices with their start and end apart: 5, of which 5 were waited for; matrix products, arithmetic and copies ran while one was open for 0% of the time, Pallas kernels for 0%

commit v1 on v0

v1 whole, which is shorter than its diff:
```python
import functools
import math

import jax
import jax.numpy as jnp
from jax import lax
from jax.experimental import pallas as pl
from jax.experimental.pallas import tpu as pltpu
from jax.sharding import PartitionSpec as P

PTS = 32768
LAGS = 128
SNAPS = 2048
MESH = pl.DeviceIdType.MESH
HIGH = lax.Precision.HIGHEST
F32 = jnp.float32
BF16 = jnp.bfloat16


def place():
    row, col, y = lax.axis_index("row"), lax.axis_index("col"), lax.axis_index("feat")
    x, z_hi = lax.rem(col, 4), lax.div(col, 4)
    core, z_lo = lax.rem(row, 2), lax.div(row, 2)
    return x, y, z_hi * 8 + z_lo, core


def device(x, y, z, core):
    return (lax.rem(z, 8) * 2 + core, lax.div(z, 8) * 4 + x, y)


def send(src, dst, send_sem, recv_sem, target):
    copy = pltpu.make_async_remote_copy(
        src_ref=src, dst_ref=dst, send_sem=send_sem, recv_sem=recv_sem,
        device_id=target, device_id_type=MESH,
    )
    copy.start()
    return copy


def greet(targets):
    barrier = pltpu.get_barrier_semaphore()
    for target in targets:
        pl.semaphore_signal(barrier, inc=1, device_id=target, device_id_type=MESH)
    pl.semaphore_wait(barrier, len(targets))


def dot(a, b, dims, precision=None):
    return lax.dot_general(
        a, b, (dims, ((), ())), precision=precision, preferred_element_type=F32
    )


def distance_kernel(
    x_ref, start_ref, dist_ref, basis_ref,
    zbuf, abuf, bbuf, part, sib, own, upbuf, downbuf, stage,
    z_send, z_recv, plane_send, plane_recv, gather_send, gather_recv,
    sib_send, sib_recv, up_send, up_recv, down_send, down_recv,
    agu_send, agu_recv, agd_send, agd_recv, st_send, st_recv,
):
    x, y, z, core = place()
    me = z * 2 + core
    row = lax.rem(z, 8) * 2 + core

    def line(t):
        return device(x, y, lax.div(t, 2), lax.rem(t, 2))

    def along_x(k):
        return device(lax.rem(x + k, 4), y, z, core)

    def along_y(k):
        return device(x, lax.rem(y + k, 4), z, core)

    sibling = device(x, y, z, 1 - core)
    above = device(x, y, lax.rem(z + 1, 16), core)
    below = device(x, y, lax.rem(z + 15, 16), core)
    greet([line(lax.rem(me + o, 32)) for o in range(1, 32)]
          + [along_x(k) for k in (1, 2, 3)] + [along_y(k) for k in (1, 2, 3)])

    def slot(t):
        z_from, core_from = lax.div(t, 2), lax.rem(t, 2)
        z_lo, z_hi = lax.rem(z_from, 8), lax.div(z_from, 8)
        return lax.div(z_lo, 2), lax.rem(z_lo, 2) * 4 + core_from * 2 + z_hi

    def columns(t):
        return pl.ds(pl.multiple_of(t * 256, 256), 256)

    big, small = slot(me)
    copies = []
    for o in range(1, 32):
        t = lax.rem(me + o, 32)
        copies.append(send(x_ref.at[:, columns(t)], zbuf.at[big, small],
                           z_send.at[o], z_recv.at[o], line(t)))
    zbuf[big, small] = x_ref[:, columns(me)]
    for copy in copies:
        copy.wait()

    giver = lax.div(row, 4) == y
    basis_slot = lax.rem(row, 4)

    def basis_copy(o):
        t = lax.rem(row + o, 16)
        return pltpu.make_async_remote_copy(
            src_ref=start_ref, dst_ref=basis_ref.at[basis_slot],
            send_sem=st_send.at[o], recv_sem=st_recv.at[basis_slot],
            device_id=(t, lax.axis_index("col"), y), device_id_type=MESH)

    @pl.when(giver)
    def _():
        for o in range(1, 16):
            basis_copy(o).start()
        basis_ref[basis_slot] = start_ref[...]

    a_copies, b_copies = [], []
    for k in (1, 2, 3):
        a_copies.append(send(zbuf.at[lax.rem(x + k, 4)], abuf.at[y, :, x],
                             plane_send.at[0, k], plane_recv.at[0, k], along_x(k)))
        b_copies.append(send(zbuf.at[lax.rem(y + k, 4)], bbuf.at[y, :, x],
                             plane_send.at[1, k], plane_recv.at[1, k], along_y(k)))
    abuf[y, :, x] = zbuf[x]
    bbuf[y, :, x] = zbuf[y]
    gathers = []
    for copy in a_copies:
        copy.wait()
    for k in (1, 2, 3):
        gathers.append(send(abuf.at[y], abuf.at[y],
                            gather_send.at[0, k], gather_recv.at[0, k], along_y(k)))
    for copy in b_copies:
        copy.wait()
    for k in (1, 2, 3):
        gathers.append(send(bbuf.at[:, :, x], bbuf.at[:, :, x],
                            gather_send.at[1, k], gather_recv.at[1, k], along_x(k)))
    for copy in gathers:
        copy.wait()

    products = jnp.zeros((512, 512), F32)
    a_norm = jnp.zeros((512, 1), F32)
    b_norm = jnp.zeros((8, 512), F32)
    for q in range(4):
        a = abuf[q].reshape(512, 256)
        b = bbuf[q].reshape(512, 256)
        products += dot(a, b, ((1,), (1,)))
        a_wide, b_wide = a.astype(F32), b.astype(F32)
        a_norm += jnp.sum(a_wide * a_wide, axis=1, keepdims=True)
        b_norm += dot(jnp.ones((8, 256), F32), b_wide * b_wide, ((1,), (1,)), HIGH)
    part[...] = (a_norm + b_norm[0:1] - 2.0 * products).reshape(2, 16, 16, 512)

    copy = send(part.at[1 - core], sib, sib_send, sib_recv, sibling)
    copy.wait()
    own[...] = part[core] + sib[...]

    def chunk(q):
        return lax.rem(q + 32, 16)

    ups, downs = [], []
    for s in range(8):
        q = chunk(z + 8 - s)
        if s == 0:
            source = own.at[q]
        else:
            ups[-1].wait_recv()
            stage[0, s] = upbuf[s - 1] + own[q]
            source = stage.at[0, s]
        ups.append(send(source, upbuf.at[s], up_send.at[s], up_recv.at[s], above))
        if s < 7:
            q = chunk(z - 7 + s)
            if s == 0:
                source = own.at[q]
            else:
                downs[-1].wait_recv()
                stage[1, s] = downbuf[s - 1] + own[q]
                source = stage.at[1, s]
            downs.append(send(source, downbuf.at[s], down_send.at[s], down_recv.at[s], below))
    ups[-1].wait_recv()
    downs[-1].wait_recv()
    dist_ref[z] = own[z] + upbuf[7] + downbuf[6]
    ag_up, ag_down = [], []
    for s in range(8):
        if s:
            ag_up[-1].wait_recv()
        q = chunk(z - s)
        ag_up.append(send(dist_ref.at[q], dist_ref.at[q], agu_send.at[s], agu_recv.at[s], above))
        if s < 7:
            if s:
                ag_down[-1].wait_recv()
            q = chunk(z + s)
            ag_down.append(send(dist_ref.at[q], dist_ref.at[q], agd_send.at[s], agd_recv.at[s], below))
    ag_up[-1].wait_recv()
    ag_down[-1].wait_recv()
    for copy in ups + downs + ag_up + ag_down:
        copy.wait_send()

    @pl.when(giver)
    def _():
        for o in range(1, 16):
            basis_copy(o).wait_send()

    for k in range(4):
        @pl.when(row != 4 * y + k)
        def _():
            pltpu.make_async_remote_copy(
                src_ref=start_ref, dst_ref=basis_ref.at[k],
                send_sem=st_send.at[0], recv_sem=st_recv.at[k],
                device_id=sibling, device_id_type=MESH).wait_recv()


def inverse_factor(gram):
    rows = lax.broadcasted_iota(jnp.int32, (32, 128), 0)
    lanes = lax.broadcasted_iota(jnp.int32, (32, 128), 1)
    work = jnp.where(lanes < 32, gram, jnp.where(lanes - 32 == rows, 1.0, 0.0))
    for k in range(31):
        top = work[k:k + 1, :]
        ratio = work[:, k:k + 1] / top[:, k:k + 1]
        work = work - jnp.where(rows > k, ratio, 0.0) * top
    diagonal = jnp.sum(jnp.where(lanes == rows, work, 0.0), axis=1, keepdims=True)
    return work[:, 32:64] / jnp.sqrt(diagonal)


def basis_kernel(
    dist_ref, start_ref, out_ref,
    ext, kern, deg, wide, outgo, income, final,
    halo_send, halo_recv, sib_send, sib_recv, deg_send, deg_recv,
    step_send, step_recv, fin_send, fin_recv,
):
    x, y, z, core = place()
    z_lo = lax.rem(z, 8)
    x_next = lax.rem(x + core, 4)

    def along_x(k):
        return device(lax.rem(x + k, 4), y, z, core)

    def along_y(k):
        return device(x, lax.rem(y + k, 4), z, core)

    y_next = lax.rem(y + 1, 4)
    sibling = device(x, y, z, 1 - core)
    down = device(x_next, y, z, 1 - core)
    right = device(x, y_next, z, core)
    diagonal = device(x_next, y_next, z, 1 - core)
    x_prev, y_prev = lax.rem(x + 3 + core, 4), lax.rem(y + 3, 4)
    up = device(x_prev, y, z, 1 - core)
    up_left = device(x_prev, y_prev, z, 1 - core)
    greet([sibling, down, up, diagonal, up_left]
          + [along_x(k) for k in (1, 2, 3)] + [along_y(k) for k in (1, 2, 3)])

    copies = [
        send(dist_ref.at[pl.ds(128, 128), :], ext.at[pl.ds(0, 128), pl.ds(128, 512)],
             halo_send.at[0], halo_recv.at[0], down),
        send(dist_ref.at[:, pl.ds(384, 128)], ext.at[pl.ds(128, 256), pl.ds(0, 128)],
             halo_send.at[1], halo_recv.at[1], right),
        send(dist_ref.at[pl.ds(128, 128), pl.ds(384, 128)], ext.at[pl.ds(0, 128), pl.ds(0, 128)],
             halo_send.at[2], halo_recv.at[2], diagonal),
    ]
    ext[128:384, 128:640] = dist_ref[...]
    for copy in copies:
        copy.wait()
    rows = lax.broadcasted_iota(jnp.int32, (384, 640), 0)
    lanes = lax.broadcasted_iota(jnp.int32, (384, 640), 1)
    first_row = jnp.where(2 * x + core == 0, 128, 0)
    first_lane = jnp.where(y == 0, 128, 0)
    run = jnp.where((rows >= first_row) & (lanes >= first_lane), ext[...], 0.0)
    stride = 1
    while stride < LAGS:
        run = run + pltpu.roll(pltpu.roll(run, stride, 0), stride, 1)
        stride *= 2
    lagged = run[128:, 128:]
    i = lax.broadcasted_iota(jnp.int32, (256, 512), 0) + (x * 512 + core * 256)
    j = lax.broadcasted_iota(jnp.int32, (256, 512), 1) + y * 512
    counts = (jnp.minimum(jnp.minimum(i, j), LAGS - 1) + 1).astype(F32)
    kern[core] = jnp.exp(-(lagged / (counts * (PTS * 0.25))))
    copy = send(kern.at[core], kern.at[core], sib_send, sib_recv, sibling)
    copy.wait()
    tile = kern[...].reshape(512, 512)

    ones = jnp.ones((8, 512), F32)
    deg[0, y] = dot(ones, tile, ((1,), (1,)), HIGH)
    deg[1, x] = dot(ones, tile, ((1,), (0,)), HIGH)
    copies = []
    for k in (1, 2, 3):
        copies.append(send(deg.at[0, y], deg.at[0, y], deg_send.at[0, k], deg_recv.at[0, k], along_y(k)))
        copies.append(send(deg.at[1, x], deg.at[1, x], deg_send.at[1, k], deg_recv.at[1, k], along_x(k)))
    for copy in copies:
        copy.wait()

    def four(ref):
        return (ref[0] + ref[1]) + (ref[2] + ref[3])

    scale_row = 1.0 / jnp.sqrt(four(deg.at[0])[0:1])
    scale_col = 1.0 / jnp.sqrt(four(deg.at[1])[0:1])

    wide[...] = jnp.zeros_like(wide)

    def gram_of(block):
        wide[0:32, :] = block
        return dot(block, wide[...], ((1,), (1,)), HIGH)

    basis = jnp.concatenate([start_ref[q] for q in range(4)], axis=1)
    pending = jnp.zeros((32, 128), F32)
    inverse = None
    for step in range(6):
        over_y = step % 2 == 0
        mine = y if over_y else x
        if over_y:
            product = dot(basis * scale_col, tile, ((1,), (1,)), HIGH) * scale_row
        else:
            product = dot(basis * scale_row, tile, ((1,), (0,)), HIGH) * scale_col
        send_gram = step in (2, 4)
        width = 640 if send_gram else 512
        income[step, mine, :, 0:512] = product
        if send_gram:
            income[step, mine, :, 512:640] = pending
        copies = []
        for k in (1, 2, 3):
            view = income.at[step, mine, :, pl.ds(0, width)]
            copies.append(send(view, view, step_send.at[step, k], step_recv.at[step, k],
                               along_y(k) if over_y else along_x(k)))
        if step in (3, 5):
            inverse = inverse_factor(gram)
        for copy in copies:
            copy.wait()
        total = four(income.at[step, :, :, pl.ds(0, width)])
        basis = total[:, :512]
        if send_gram:
            gram = total[:, 512:]
        if step in (3, 5):
            basis = dot(inverse, basis, ((1,), (0,)), HIGH)
        if step in (1, 3, 5):
            pending = gram_of(basis)

    owner = lax.div(z_lo, 2)
    final[0, y] = pending
    copies = []
    for k in (1, 2, 3):
        copies.append(send(final.at[0, y], final.at[0, y], fin_send.at[k], fin_recv.at[k], along_y(k)))

    def row_copy(k):
        return pltpu.make_async_remote_copy(
            src_ref=final.at[1, 0], dst_ref=final.at[1, 0],
            send_sem=fin_send.at[3 + k], recv_sem=fin_recv.at[0],
            device_id=along_y(k), device_id_type=MESH)

    @pl.when(y == owner)
    def _():
        for q in range(4):
            @pl.when(lax.rem(z_lo, 2) * 2 + core == q)
            def _():
                final[1, 0] = basis[:, q * 128:(q + 1) * 128]
        for k in (1, 2, 3):
            row_copy(k).start()
        for k in (1, 2, 3):
            row_copy(k).wait_send()

    for copy in copies:
        copy.wait()
    inverse = inverse_factor(four(final.at[0]))

    @pl.when(y != owner)
    def _():
        row_copy(1).wait_recv()

    out_ref[...] = dot(inverse, final[1, 0], ((1,), (0,)), HIGH) * math.sqrt(SNAPS)


VMEM = pl.BlockSpec(memory_space=pltpu.VMEM)
DMA = pltpu.SemaphoreType.DMA


def body(snapshots, start_block):
    dist, start = pl.pallas_call(
        distance_kernel,
        out_shape=(jax.ShapeDtypeStruct((16, 16, 512), F32),
                   jax.ShapeDtypeStruct((4, 32, 128), F32)),
        in_specs=[VMEM, VMEM],
        out_specs=(VMEM, VMEM),
        scratch_shapes=[
            pltpu.VMEM((4, 8, 16, 256), BF16),
            pltpu.VMEM((4, 8, 4, 16, 256), BF16),
            pltpu.VMEM((4, 8, 4, 16, 256), BF16),
            pltpu.VMEM((2, 16, 16, 512), F32),
            pltpu.VMEM((16, 16, 512), F32),
            pltpu.VMEM((16, 16, 512), F32),
            pltpu.VMEM((8, 16, 512), F32),
            pltpu.VMEM((7, 16, 512), F32),
            pltpu.VMEM((2, 8, 16, 512), F32),
            DMA((32,)), DMA((32,)), DMA((2, 4)), DMA((2, 4)), DMA((2, 4)), DMA((2, 4)),
            DMA, DMA, DMA((8,)), DMA((8,)), DMA((7,)), DMA((7,)),
            DMA((8,)), DMA((8,)), DMA((7,)), DMA((7,)), DMA((16,)), DMA((4,)),
        ],
        compiler_params=pltpu.CompilerParams(
            collective_id=1, has_side_effects=True, vmem_limit_bytes=40 << 20),
        name="distances",
    )(snapshots, start_block.T)
    out = pl.pallas_call(
        basis_kernel,
        out_shape=jax.ShapeDtypeStruct((32, 128), F32),
        in_specs=[VMEM, VMEM],
        out_specs=VMEM,
        scratch_shapes=[
            pltpu.VMEM((384, 640), F32),
            pltpu.VMEM((2, 256, 512), F32),
            pltpu.VMEM((2, 4, 8, 512), F32),
            pltpu.VMEM((128, 512), F32),
            pltpu.VMEM((8, 128), F32),
            pltpu.VMEM((6, 4, 32, 640), F32),
            pltpu.VMEM((2, 4, 32, 128), F32),
            DMA((3,)), DMA((3,)), DMA, DMA, DMA((2, 4)), DMA((2, 4)),
            DMA((6, 4)), DMA((6, 4)), DMA((7,)), DMA((4,)),
        ],
        compiler_params=pltpu.CompilerParams(
            collective_id=2, has_side_effects=True, vmem_limit_bytes=40 << 20),
        name="subspace",
    )(dist.reshape(256, 512), start)
    return out.T


def solution(mesh):
    placed = (P(("row", "col"), "feat"), P("row", None))
    return jax.shard_map(
        body, mesh=mesh, in_specs=placed, out_specs=P("row", None), check_vma=False
    )
```

time: 554 us -> 173 us (0.31)
  the two profiles are of different devices: /device:TPU:1 before, /device:TPU:32 now
where the time goes in v1:
time: 173 us; the launch traced here: 172 us
  Pallas kernels  170 us (98%)
  local copies, waits for them, and re-layouts  2.27 us (1%)
    pallas_call x1, Pallas kernels, body(): pl.pallas_call(distance_kernel, out_shape=(jax.ShapeDtypeStruct((16, 16,...  105 us
    pallas_call x1, Pallas kernels, body(): pl.pallas_call(basis_kernel, out_shape=jax.ShapeDtypeStruct((32, 128), F3...  65.1 us

profile of v1, /device:TPU:32, one launch (start us, length us, event | category | flops | bytes accessed | tf_op | source)
XLA Modules:
  0.0 172.4 jit_solution(15512088719363713019)
XLA Ops:
  0.0 0.0 copy-start
  0.0 0.9 copy-done
  1.0 0.0 copy-start.1
  1.0 0.7 copy-done.1
  1.7 105.0 %distances.1 = (f32[16,16,512]{2,1,0:T(8,128)S(1)}, f32[4,32,128]{2,1,0:T(8,128)S(1)}) custom-call(bf16[16,8192]{1,0:T(8,128)(2,1)S(1)} %copy-done, f32[32,128]{1,0:T(8,128)S(1)} %bitcast.5), custom_call_target="tpu_custom_call" | custom-call | tf_op jit(solution)/shard_map/distances/pallas_call | solution.py:368
  106.7 65.1 %subspace.1 = f32[32,128]{1,0:T(8,128)S(1)} custom-call(f32[256,512]{1,0:T(8,128)S(1)} %bitcast.3, f32[4,32,128]{2,1,0:T(8,128)S(1)} %get-tuple-element.8.start_ref), custom_call_target="tpu_custom_call" | custom-call | tf_op jit(solution)/shard_map/subspace/pallas_call | solution.py:392
  171.8 0.6 copy.4
Async XLA Ops:
  0.0 0.9 copy-start
  1.0 0.7 copy-start.1

commit v2 on v0

v2 whole, which is shorter than its diff:
```python
import math

import jax
import jax.numpy as jnp
from jax import lax
from jax.experimental import pallas as pl
from jax.experimental.pallas import tpu as pltpu
from jax.sharding import PartitionSpec as P

PTS = 32768
LAGS = 128
SNAPS = 2048
PLANES = (1, 5, 9, 13)
MESH = pl.DeviceIdType.MESH
HIGH = lax.Precision.HIGHEST
F32 = jnp.float32
BF16 = jnp.bfloat16


def device(x, y, z, core):
    return (lax.rem(z, 8) * 2 + core, lax.div(z, 8) * 4 + x, y)


def remote(src, dst, send_sem, recv_sem, target):
    return pltpu.make_async_remote_copy(
        src_ref=src, dst_ref=dst, send_sem=send_sem, recv_sem=recv_sem,
        device_id=target, device_id_type=MESH,
    )


def send(*args):
    copy = remote(*args)
    copy.start()
    return copy


def dot(a, b, dims, precision=None):
    return lax.dot_general(
        a, b, (dims, ((), ())), precision=precision, preferred_element_type=F32
    )


def parts(value, count):
    out = []
    for _ in range(count):
        out.append(value.astype(BF16))
        value = value - out[-1].astype(F32)
    return out


def inverse_factor(gram):
    rows = lax.broadcasted_iota(jnp.int32, (32, 128), 0)
    lanes = lax.broadcasted_iota(jnp.int32, (32, 128), 1)
    work = jnp.where(lanes < 32, gram, jnp.where(lanes - 32 == rows, 1.0, 0.0))
    for k in range(31):
        top = work[k:k + 1, :]
        ratio = work[:, k:k + 1] / top[:, k:k + 1]
        work = work - jnp.where(rows > k, ratio, 0.0) * top
    diagonal = jnp.sum(jnp.where(lanes == rows, work, 0.0), axis=1, keepdims=True)
    return work[:, 32:64] / jnp.sqrt(diagonal)


def four(ref):
    return (ref[0] + ref[1]) + (ref[2] + ref[3])


def kernel(
    x_ref, start_ref, out_ref,
    zbuf, abuf, bbuf, part, sib, own, rsbuf, total, dist, start,
    ext, kern_hi, kern_lo, deg_row, deg_col, wide, income, grams, last, last_rows, last_grams,
    z_send, z_recv, plane_send, plane_recv, gather_send, gather_recv,
    sib_send, sib_recv, rs_send, rs_recv, ag_send, ag_recv, st_send, st_recv,
    halo_send, halo_recv, core_send, core_recv, deg_send, deg_recv,
    step_send, step_recv, gram_send, gram_recv, fin_send, fin_recv, row_send, row_recv,
):
    row, col, y = lax.axis_index("row"), lax.axis_index("col"), lax.axis_index("feat")
    x, z_hi = lax.rem(col, 4), lax.div(col, 4)
    core, z_lo = lax.rem(row, 2), lax.div(row, 2)
    z = z_hi * 8 + z_lo
    me = z * 2 + core
    group = lax.div(z, 4)
    iterates = lax.rem(z, 4) == 1

    def line(t):
        return device(x, y, lax.div(t, 2), lax.rem(t, 2))

    def along_x(k, c=core):
        return device(lax.rem(x + k, 4), y, z, c)

    def along_y(k, c=core):
        return device(x, lax.rem(y + k, 4), z, c)

    sibling = device(x, y, z, 1 - core)
    barrier = pltpu.get_barrier_semaphore()
    partners = ([line(lax.rem(me + o, 32)) for o in range(1, 32)]
                + [along_x(k) for k in (1, 2, 3)] + [along_y(k) for k in (1, 2, 3)])
    for target in partners:
        pl.semaphore_signal(barrier, inc=1, device_id=target, device_id_type=MESH)
    pl.semaphore_wait(barrier, len(partners))

    def columns(t, h):
        return pl.ds(pl.multiple_of(t * 256 + h * 128, 128), 128)

    big, small = lax.div(z_lo, 2), lax.rem(z_lo, 2) * 4 + core * 2 + z_hi
    for h in (0, 1):
        for o in range(1, 32):
            t = lax.rem(me + o, 32)
            send(x_ref.at[:, columns(t, h)], zbuf.at[h, big, small],
                 z_send.at[h, o], z_recv.at[h, o], line(t))
        zbuf[h, big, small] = x_ref[:, columns(me, h)]

    giver = lax.div(row, 4) == y
    basis_slot = lax.rem(row, 4)

    def basis_copy(n, t):
        return remote(start_ref, start.at[basis_slot], st_send.at[n], st_recv.at[basis_slot],
                      (t, col, y))

    for n, t in enumerate((2, 3, 10, 11)):
        @pl.when(giver & (row != t))
        def _():
            basis_copy(n, t).start()

    @pl.when(giver)
    def _():
        start[basis_slot] = start_ref[...]

    first = []
    for h in (0, 1):
        for o in range(1, 32):
            remote(x_ref.at[:, columns(0, h)], zbuf.at[h, 0, 0],
                   z_send.at[h, o], z_recv.at[h, o], sibling).wait()
        pairs = []
        for k in (1, 2, 3):
            pairs.append((
                send(zbuf.at[h, lax.rem(x + k, 4)], abuf.at[h, y, :, x],
                     plane_send.at[h, 0, k], plane_recv.at[h, 0, k], along_x(k)),
                send(zbuf.at[h, lax.rem(y + k, 4)], bbuf.at[h, y, :, x],
                     plane_send.at[h, 1, k], plane_recv.at[h, 1, k], along_y(k))))
        first.append(pairs)
        abuf[h, y, :, x] = zbuf[h, x]
        bbuf[h, y, :, x] = zbuf[h, y]
    gathers = []
    for h in (0, 1):
        group_copies = []
        for copy, _ in first[h]:
            copy.wait()
        for k in (1, 2, 3):
            group_copies.append(send(abuf.at[h, y], abuf.at[h, y],
                                     gather_send.at[h, 0, k], gather_recv.at[h, 0, k], along_y(k)))
        for _, copy in first[h]:
            copy.wait()
        for k in (1, 2, 3):
            group_copies.append(send(bbuf.at[h, :, :, x], bbuf.at[h, :, :, x],
                                     gather_send.at[h, 1, k], gather_recv.at[h, 1, k], along_x(k)))
        gathers.append(group_copies)

    for h in (0, 1):
        for copy in gathers[h]:
            copy.wait()
        b = jnp.concatenate([bbuf[h, q].reshape(512, 128) for q in range(4)], axis=1)
        b_wide = b.astype(F32)
        ones = jnp.ones((16, 512), BF16)
        b_norm = sum(dot(ones, p, ((1,), (1,))) for p in parts(b_wide * b_wide, 2))[0:1]
        for half in (1 - core, core):
            a = jnp.concatenate(
                [abuf[h, q, pl.ds(half * 4, 4)].reshape(256, 128) for q in range(4)], axis=1)
            a_wide = a.astype(F32)
            a_norm = jnp.sum(a_wide * a_wide, axis=1, keepdims=True)
            value = (a_norm + b_norm - 2.0 * dot(a, b, ((1,), (1,)))).reshape(4, 4, 16, 512)
            if h == 1:
                value = value + part[half]
            part[half] = value
            if h == 1 and half is not core:
                core_sums = [send(part.at[half, n], sib.at[n], sib_send.at[n], sib_recv.at[n], sibling)
                             for n in range(4)]

    def scatter(n, i, q):
        return remote(own.at[n, i], rsbuf.at[z], rs_send.at[0], rs_recv.at[0],
                      device(x, y, q, core))

    for n in range(4):
        core_sums[n].wait()
        own[n] = part[core, n] + sib[n]
        for i in range(4):
            q = n * 4 + i

            @pl.when(z != q)
            def _():
                scatter(n, i, q).start()

            @pl.when(z == q)
            def _():
                rsbuf[q] = own[n, i]
    remote(rsbuf.at[pl.ds(0, 15)], rsbuf.at[pl.ds(0, 15)], rs_send.at[0], rs_recv.at[0], sibling).wait()
    chunk = rsbuf[0]
    for q in range(1, 16):
        chunk = chunk + rsbuf[q]
    total[...] = chunk

    my_rows = pl.ds(pl.multiple_of(z * 16, 16), 16)

    def gather(n, p):
        return remote(total, dist.at[my_rows, :], ag_send.at[n], ag_recv.at[0], device(x, y, p, core))

    for n, p in enumerate(PLANES):
        @pl.when(z != p)
        def _():
            gather(n, p).start()

    @pl.when(iterates)
    def _():
        dist[my_rows, :] = total[...]
        remote(dist.at[pl.ds(0, 240), :], dist.at[pl.ds(0, 240), :],
               ag_send.at[4], ag_recv.at[0], sibling).wait_recv()

        x_next, y_next = lax.rem(x + core, 4), lax.rem(y + 1, 4)
        halo = [
            send(dist.at[pl.ds(128, 128), :], ext.at[pl.ds(0, 128), pl.ds(128, 512)],
                 halo_send.at[0], halo_recv.at[0], device(x_next, y, z, 1 - core)),
            send(dist.at[:, pl.ds(384, 128)], ext.at[pl.ds(128, 256), pl.ds(0, 128)],
                 halo_send.at[1], halo_recv.at[1], device(x, y_next, z, core)),
            send(dist.at[pl.ds(128, 128), pl.ds(384, 128)], ext.at[pl.ds(0, 128), pl.ds(0, 128)],
                 halo_send.at[2], halo_recv.at[2], device(x_next, y_next, z, 1 - core)),
        ]
        ext[128:384, 128:640] = dist[...]
        for copy in halo:
            copy.wait()
        rows = lax.broadcasted_iota(jnp.int32, (384, 640), 0)
        lanes = lax.broadcasted_iota(jnp.int32, (384, 640), 1)
        first_row = jnp.where(2 * x + core == 0, 128, 0)
        first_lane = jnp.where(y == 0, 128, 0)
        run = jnp.where((rows >= first_row) & (lanes >= first_lane), ext[...], 0.0)
        stride = 1
        while stride < LAGS:
            run = run + pltpu.roll(pltpu.roll(run, stride, 0), stride, 1)
            stride *= 2
        lagged = run[128:, 128:]
        i = lax.broadcasted_iota(jnp.int32, (256, 512), 0) + (x * 512 + core * 256)
        j = lax.broadcasted_iota(jnp.int32, (256, 512), 1) + y * 512
        counts = (jnp.minimum(jnp.minimum(i, j), LAGS - 1) + 1).astype(F32)
        half_tile = jnp.exp(-(lagged / (counts * (PTS * 0.25))))
        half_hi, half_lo = parts(half_tile, 2)
        my_half = pl.ds(pl.multiple_of(core * 256, 256), 256)
        kern_hi[my_half, :] = half_hi
        kern_lo[my_half, :] = half_lo
        swaps = [send(ref.at[my_half, :], ref.at[my_half, :], core_send.at[n], core_recv.at[n], sibling)
                 for n, ref in enumerate((kern_hi, kern_lo))]

        ones = jnp.ones((8, 512), F32)
        deg_row[core, y] = dot(ones, half_tile, ((1,), (1,)), HIGH)
        deg_col[core, x] = dot(ones[:, :256], half_tile, ((1,), (0,)), HIGH)
        copies = []
        for c in (0, 1):
            for k in range(4):
                if c == 0 and k == 0:
                    continue
                c_to = lax.rem(core + c, 2)
                view = deg_row.at[core, y]
                copies.append(send(view, view, deg_send.at[0, c, k], deg_recv.at[0, c, k], along_y(k, c_to)))
                view = deg_col.at[core, x]
                copies.append(send(view, view, deg_send.at[1, c, k], deg_recv.at[1, c, k], along_x(k, c_to)))
        for copy in swaps:
            copy.wait()
        tile_hi, tile_lo = kern_hi[...], kern_lo[...]
        for copy in copies:
            copy.wait()
        row_sums = jnp.concatenate([four(deg_row.at[0]), four(deg_row.at[1])], axis=1)[0:1]
        scale_row = 1.0 / jnp.sqrt(row_sums)
        scale_col = 1.0 / jnp.sqrt((four(deg_col.at[0]) + four(deg_col.at[1]))[0:1])
        wide[...] = jnp.zeros_like(wide)

        def gram_of(block):
            wide[0:32, :] = block
            return dot(block, wide[...], ((1,), (1,)), HIGH)

        for k in range(4):
            @pl.when(row != 4 * y + k)
            def _():
                remote(start_ref, start.at[k], st_send.at[4], st_recv.at[k], sibling).wait_recv()
        mine = [start[k] for k in range(4)]
        basis = jnp.concatenate(mine, axis=1)
        inverse = None
        gram_copies = None
        for step in range(6):
            over_y = step % 2 == 0
            at = y if over_y else x
            scaled = parts(basis * (scale_col if over_y else scale_row), 3)
            dims = ((1,), (1,)) if over_y else ((1,), (0,))
            high = dot(jnp.concatenate(scaled, axis=0), tile_hi, dims)
            low = dot(jnp.concatenate(scaled[:2], axis=0), tile_lo, dims)
            product = high[:32] + ((high[32:64] + low[:32]) + (high[64:] + low[32:]))
            income[step, at] = product * (scale_row if over_y else scale_col)
            copies = []
            for k in (1, 2, 3):
                view = income.at[step, at]
                copies.append(send(view, view, step_send.at[step, k], step_recv.at[step, k],
                                   along_y(k) if over_y else along_x(k)))
            if step in (2, 4):
                n = step // 2 - 1
                grams[n, y] = gram_of(basis)
                gram_copies = [send(grams.at[n, y], grams.at[n, y], gram_send.at[n, k],
                                    gram_recv.at[n, k], along_y(k)) for k in (1, 2, 3)]
            if step in (3, 5):
                for copy in gram_copies:
                    copy.wait()
                inverse = inverse_factor(four(grams.at[step // 2 - 1]))
            for copy in copies:
                copy.wait()
            basis = four(income.at[step])
            if step in (3, 5):
                basis = dot(inverse, basis, ((1,), (0,)), HIGH)

        last[...] = basis
        last_grams[y] = gram_of(basis)
        owner = lax.div(y, 2) == lax.rem(group, 2)
        waits = []
        for k in range(4):
            for i in range(4):
                z_to = group * 4 + lax.rem(1 + i, 4)
                target = device(x, lax.rem(y + k, 4), z_to, core)
                if k or i:
                    waits.append(send(last_grams.at[y], last_grams.at[y], fin_send.at[k, i],
                                      fin_recv.at[y], target))

        def row_copy(k, i):
            lane = pl.multiple_of((i * 2 + core) * 128, 128)
            return remote(last.at[:, pl.ds(lane, 128)], last_rows, row_send.at[k, i], row_recv.at[0],
                          device(x, lax.rem(y + k, 4), z_hi * 8 + 2 * y + i, core))

        for k in range(4):
            for i in range(2):
                to_self = (k == 0) & (z_lo == 2 * y + i)

                @pl.when(owner & jnp.logical_not(to_self))
                def _():
                    row_copy(k, i).start()

                if k == 0:
                    @pl.when(owner & to_self)
                    def _():
                        lane = pl.multiple_of((i * 2 + core) * 128, 128)
                        last_rows[...] = last[:, pl.ds(lane, 128)]
        for copy in waits:
            copy.wait_send()
        for k in range(4):
            for i in range(2):
                to_self = (k == 0) & (z_lo == 2 * y + i)

                @pl.when(owner & jnp.logical_not(to_self))
                def _():
                    row_copy(k, i).wait_send()

    for q in range(4):
        @pl.when(jnp.logical_not(iterates & (y == q)))
        def _():
            remote(last_grams.at[q], last_grams.at[q], fin_send.at[0, 0], fin_recv.at[q], sibling).wait_recv()
    inverse = inverse_factor(four(last_grams))

    @pl.when(jnp.logical_not(iterates & (y == lax.div(z_lo, 2))))
    def _():
        remote(last_rows, last_rows, row_send.at[0, 0], row_recv.at[0], sibling).wait_recv()

    out_ref[...] = dot(inverse, last_rows[...], ((1,), (0,)), HIGH) * math.sqrt(SNAPS)

    for n, t in enumerate((2, 3, 10, 11)):
        @pl.when(giver & (row != t))
        def _():
            basis_copy(n, t).wait_send()
    for n, p in enumerate(PLANES):
        @pl.when(z != p)
        def _():
            gather(n, p).wait_send()


VMEM = pl.BlockSpec(memory_space=pltpu.VMEM)
DMA = pltpu.SemaphoreType.DMA


def body(snapshots, start_block):
    out = pl.pallas_call(
        kernel,
        out_shape=jax.ShapeDtypeStruct((32, 128), F32),
        in_specs=[VMEM, VMEM],
        out_specs=VMEM,
        scratch_shapes=[
            pltpu.VMEM((2, 4, 8, 16, 128), BF16),
            pltpu.VMEM((2, 4, 8, 4, 16, 128), BF16),
            pltpu.VMEM((2, 4, 8, 4, 16, 128), BF16),
            pltpu.VMEM((2, 4, 4, 16, 512), F32),
            pltpu.VMEM((4, 4, 16, 512), F32),
            pltpu.VMEM((4, 4, 16, 512), F32),
            pltpu.VMEM((16, 16, 512), F32),
            pltpu.VMEM((16, 512), F32),
            pltpu.VMEM((256, 512), F32),
            pltpu.VMEM((4, 32, 128), F32),
            pltpu.VMEM((384, 640), F32),
            pltpu.VMEM((512, 512), BF16),
            pltpu.VMEM((512, 512), BF16),
            pltpu.VMEM((2, 4, 8, 256), F32),
            pltpu.VMEM((2, 4, 8, 512), F32),
            pltpu.VMEM((128, 512), F32),
            pltpu.VMEM((6, 4, 32, 512), F32),
            pltpu.VMEM((2, 4, 32, 128), F32),
            pltpu.VMEM((32, 512), F32),
            pltpu.VMEM((32, 128), F32),
            pltpu.VMEM((4, 32, 128), F32),
            DMA((2, 32)), DMA((2, 32)), DMA((2, 2, 4)), DMA((2, 2, 4)), DMA((2, 2, 4)), DMA((2, 2, 4)),
            DMA((4,)), DMA((4,)), DMA((1,)), DMA((1,)), DMA((5,)), DMA((1,)), DMA((5,)), DMA((4,)),
            DMA((3,)), DMA((3,)), DMA((2,)), DMA((2,)), DMA((2, 2, 4)), DMA((2, 2, 4)),
            DMA((6, 4)), DMA((6, 4)), DMA((2, 4)), DMA((2, 4)), DMA((4, 4)), DMA((4,)),
            DMA((4, 2)), DMA((1,)),
        ],
        compiler_params=pltpu.CompilerParams(
            collective_id=1, has_side_effects=True, vmem_limit_bytes=48 << 20),
        name="subspace",
    )(snapshots, start_block.T)
    return out.T


def solution(mesh):
    placed = (P(("row", "col"), "feat"), P("row", None))
    return jax.shard_map(
        body, mesh=mesh, in_specs=placed, out_specs=P("row", None), check_vma=False
    )
```

time: 554 us -> 146 us (0.26)
  the two profiles are of different devices: /device:TPU:1 before, /device:TPU:4 now
where the time goes in v2:
time: 146 us; the launch traced here: 145 us
  Pallas kernels  143 us (98%)
  local copies, waits for them, and re-layouts  2.27 us (2%)
    pallas_call x1, Pallas kernels, body(): pl.pallas_call(kernel, out_shape=jax.ShapeDtypeStruct((32, 128), F32), in...  143 us

profile of v2, /device:TPU:4, one launch (start us, length us, event | category | flops | bytes accessed | tf_op | source)
XLA Modules:
  0.0 145.4 jit_solution(9286499112242451659)
XLA Ops:
  0.0 0.0 copy-start
  0.0 0.9 copy-done
  1.0 0.0 copy-start.1
  1.0 0.7 copy-done.1
  1.7 143.1 %subspace.1 = f32[32,128]{1,0:T(8,128)S(1)} custom-call(bf16[16,8192]{1,0:T(8,128)(2,1)S(1)} %copy-done, f32[32,128]{1,0:T(8,128)S(1)} %bitcast.3), custom_call_target="tpu_custom_call" | custom-call | tf_op jit(solution)/shard_map/subspace/pallas_call | solution.py:381
  144.8 0.6 copy.4
Async XLA Ops:
  0.0 0.9 copy-start
  1.0 0.7 copy-start.1

commit v3 on v2

--- a/solution.py
+++ b/solution.py
@@ -52,10 +52,17 @@
     rows = lax.broadcasted_iota(jnp.int32, (32, 128), 0)
     lanes = lax.broadcasted_iota(jnp.int32, (32, 128), 1)
     work = jnp.where(lanes < 32, gram, jnp.where(lanes - 32 == rows, 1.0, 0.0))
-    for k in range(31):
-        top = work[k:k + 1, :]
-        ratio = work[:, k:k + 1] / top[:, k:k + 1]
-        work = work - jnp.where(rows > k, ratio, 0.0) * top
+    for k in range(0, 32, 2):
+        top, next_top = work[k:k + 1, :], work[k + 1:k + 2, :]
+        left, right = work[:, k:k + 1], work[:, k + 1:k + 2]
+        scale = 1.0 / top[:, k:k + 1]
+        ratio = left * scale
+        step = next_top[:, k:k + 1] * scale
+        next_top = next_top - step * top
+        next_ratio = (right - ratio * top[:, k + 1:k + 2]) / next_top[:, k + 1:k + 2]
+        first = jnp.where(rows > k, ratio, 0.0)
+        second = jnp.where(rows > k + 1, next_ratio, 0.0)
+        work = (work - first * top) - second * next_top
     diagonal = jnp.sum(jnp.where(lanes == rows, work, 0.0), axis=1, keepdims=True)
     return work[:, 32:64] / jnp.sqrt(diagonal)
 
@@ -68,7 +75,7 @@
     x_ref, start_ref, out_ref,
     zbuf, abuf, bbuf, part, sib, own, rsbuf, total, dist, start,
     ext, kern_hi, kern_lo, deg_row, deg_col, wide, income, grams, last, last_rows, last_grams,
-    z_send, z_recv, plane_send, plane_recv, gather_send, gather_recv,
+    local_sem, z_send, z_recv, plane_send, plane_recv, gather_send, gather_recv,
     sib_send, sib_recv, rs_send, rs_recv, ag_send, ag_recv, st_send, st_recv,
     halo_send, halo_recv, core_send, core_recv, deg_send, deg_recv,
     step_send, step_recv, gram_send, gram_recv, fin_send, fin_recv, row_send, row_recv,
@@ -92,7 +99,8 @@
 
     sibling = device(x, y, z, 1 - core)
     barrier = pltpu.get_barrier_semaphore()
-    partners = ([line(lax.rem(me + o, 32)) for o in range(1, 32)]
+    far_first = sorted(range(1, 32), key=lambda o: -min(o, 32 - o))
+    partners = ([line(lax.rem(me + o, 32)) for o in far_first]
                 + [along_x(k) for k in (1, 2, 3)] + [along_y(k) for k in (1, 2, 3)])
     for target in partners:
         pl.semaphore_signal(barrier, inc=1, device_id=target, device_id_type=MESH)
@@ -102,12 +110,21 @@
         return pl.ds(pl.multiple_of(t * 256 + h * 128, 128), 128)
 
     big, small = lax.div(z_lo, 2), lax.rem(z_lo, 2) * 4 + core * 2 + z_hi
+    halves = []
     for h in (0, 1):
-        for o in range(1, 32):
+        if h:
+            for copy in halves[0]:
+                copy.wait_send()
+        copies = []
+        for o in far_first:
             t = lax.rem(me + o, 32)
-            send(x_ref.at[:, columns(t, h)], zbuf.at[h, big, small],
-                 z_send.at[h, o], z_recv.at[h, o], line(t))
-        zbuf[h, big, small] = x_ref[:, columns(me, h)]
+            copies.append(send(x_ref.at[:, columns(t, h)], zbuf.at[h, big, small],
+                               z_send.at[h, o], z_recv.at[h, o], line(t)))
+        halves.append(copies)
+    here = [pltpu.make_async_copy(x_ref.at[:, columns(me, h)], zbuf.at[h, big, small], local_sem.at[h])
+            for h in (0, 1)]
+    for copy in here:
+        copy.start()
 
     giver = lax.div(row, 4) == y
     basis_slot = lax.rem(row, 4)
@@ -116,20 +133,24 @@
         return remote(start_ref, start.at[basis_slot], st_send.at[n], st_recv.at[basis_slot],
                       (t, col, y))
 
-    for n, t in enumerate((2, 3, 10, 11)):
+    for n, t in enumerate((2, 10)):
         @pl.when(giver & (row != t))
         def _():
             basis_copy(n, t).start()
 
     @pl.when(giver)
     def _():
-        start[basis_slot] = start_ref[...]
+        copy = pltpu.make_async_copy(start_ref, start.at[basis_slot], local_sem.at[2])
+        copy.start()
+        copy.wait()
 
     first = []
     for h in (0, 1):
-        for o in range(1, 32):
-            remote(x_ref.at[:, columns(0, h)], zbuf.at[h, 0, 0],
-                   z_send.at[h, o], z_recv.at[h, o], sibling).wait()
+        here[h].wait()
+        for copy in halves[h]:
+            if h:
+                copy.wait_send()
+            copy.wait_recv()
         pairs = []
         for k in (1, 2, 3):
             pairs.append((
@@ -175,23 +196,13 @@
                 core_sums = [send(part.at[half, n], sib.at[n], sib_send.at[n], sib_recv.at[n], sibling)
                              for n in range(4)]
 
-    def scatter(n, i, q):
-        return remote(own.at[n, i], rsbuf.at[z], rs_send.at[0], rs_recv.at[0],
-                      device(x, y, q, core))
-
     for n in range(4):
         core_sums[n].wait()
-        own[n] = part[core, n] + sib[n]
-        for i in range(4):
-            q = n * 4 + i
-
-            @pl.when(z != q)
-            def _():
-                scatter(n, i, q).start()
-
-            @pl.when(z == q)
-            def _():
-                rsbuf[q] = own[n, i]
+        own[pl.ds(n * 4, 4)] = part[core, n] + sib[n]
+    for o in sorted(range(1, 16), key=lambda o: -min(o, 16 - o)):
+        q = lax.rem(z + o, 16)
+        send(own.at[q], rsbuf.at[z], rs_send.at[0], rs_recv.at[0], device(x, y, q, core))
+    rsbuf[z] = own[z]
     remote(rsbuf.at[pl.ds(0, 15)], rsbuf.at[pl.ds(0, 15)], rs_send.at[0], rs_recv.at[0], sibling).wait()
     chunk = rsbuf[0]
     for q in range(1, 16):
@@ -231,11 +242,15 @@
         first_row = jnp.where(2 * x + core == 0, 128, 0)
         first_lane = jnp.where(y == 0, 128, 0)
         run = jnp.where((rows >= first_row) & (lanes >= first_lane), ext[...], 0.0)
-        stride = 1
-        while stride < LAGS:
-            run = run + pltpu.roll(pltpu.roll(run, stride, 0), stride, 1)
-            stride *= 2
-        lagged = run[128:, 128:]
+        stride = LAGS // 2
+        while stride >= 1:
+            turned = pltpu.roll(run, stride, 1)
+            if stride >= 8:
+                run = run[stride:] + turned[:-stride]
+            else:
+                run = run + pltpu.roll(turned, stride, 0)
+            stride //= 2
+        lagged = run[8:, 128:]
         i = lax.broadcasted_iota(jnp.int32, (256, 512), 0) + (x * 512 + core * 256)
         j = lax.broadcasted_iota(jnp.int32, (256, 512), 1) + y * 512
         counts = (jnp.minimum(jnp.minimum(i, j), LAGS - 1) + 1).astype(F32)
@@ -244,42 +259,67 @@
         my_half = pl.ds(pl.multiple_of(core * 256, 256), 256)
         kern_hi[my_half, :] = half_hi
         kern_lo[my_half, :] = half_lo
-        swaps = [send(ref.at[my_half, :], ref.at[my_half, :], core_send.at[n], core_recv.at[n], sibling)
+        swaps = [remote(ref.at[my_half, :], ref.at[my_half, :], core_send.at[n], core_recv.at[n], sibling)
                  for n, ref in enumerate((kern_hi, kern_lo))]
+
+        @pl.when(core == 1)
+        def _():
+            for copy in swaps:
+                copy.start()
 
         ones = jnp.ones((8, 512), F32)
         deg_row[core, y] = dot(ones, half_tile, ((1,), (1,)), HIGH)
         deg_col[core, x] = dot(ones[:, :256], half_tile, ((1,), (0,)), HIGH)
-        copies = []
-        for c in (0, 1):
+
+        def degree_copies(k):
+            row_view, col_view = deg_row.at[core, y], deg_col.at[core, x]
+            return (remote(row_view, row_view, deg_send.at[0, k], deg_recv.at[0, core, k], along_y(k, 0)),
+                    remote(col_view, col_view, deg_send.at[1, k], deg_recv.at[1, core, k], along_x(k, 0)))
+
+        @pl.when(core == 1)
+        def _():
             for k in range(4):
-                if c == 0 and k == 0:
-                    continue
-                c_to = lax.rem(core + c, 2)
-                view = deg_row.at[core, y]
-                copies.append(send(view, view, deg_send.at[0, c, k], deg_recv.at[0, c, k], along_y(k, c_to)))
-                view = deg_col.at[core, x]
-                copies.append(send(view, view, deg_send.at[1, c, k], deg_recv.at[1, c, k], along_x(k, c_to)))
-        for copy in swaps:
-            copy.wait()
+                for copy in degree_copies(k):
+                    copy.start()
+            for copy in swaps:
+                copy.wait_send()
+            for k in range(4):
+                for copy in degree_copies(k):
+                    copy.wait_send()
+
+    @pl.when(iterates & (core == 0))
+    def _():
+        def degree_copy(n, c, k):
+            ref = (deg_row, deg_col)[n].at[c, 0]
+            return remote(ref, ref, deg_send.at[n, k], deg_recv.at[n, c, k], sibling)
+
+        for k in (1, 2, 3):
+            for n, ref, target in ((0, deg_row.at[0, y], along_y(k)), (1, deg_col.at[0, x], along_x(k))):
+                remote(ref, ref, deg_send.at[n, k], deg_recv.at[n, 0, k], target).start()
+        wide[...] = jnp.zeros_like(wide)
+
+        def gram_of(block):
+            wide[0:32, :] = block
+            return dot(block, wide[...], ((1,), (1,)), HIGH)
+
+        for k in range(4):
+            @pl.when(row != 4 * y + k)
+            def _():
+                remote(start_ref, start.at[k], st_send.at[2], st_recv.at[k], sibling).wait_recv()
+        mine = [start[k].T for k in range(4)]
+        basis = jnp.concatenate(mine, axis=1)
+        other_half = pl.ds(256, 256)
+        for n, ref in enumerate((kern_hi, kern_lo)):
+            remote(ref.at[other_half, :], ref.at[other_half, :], core_send.at[n], core_recv.at[n], sibling).wait_recv()
         tile_hi, tile_lo = kern_hi[...], kern_lo[...]
-        for copy in copies:
-            copy.wait()
+        for n in (0, 1):
+            for k in (1, 2, 3):
+                degree_copy(n, 0, k).wait()
+            for k in range(4):
+                degree_copy(n, 1, k).wait_recv()
         row_sums = jnp.concatenate([four(deg_row.at[0]), four(deg_row.at[1])], axis=1)[0:1]
         scale_row = 1.0 / jnp.sqrt(row_sums)
         scale_col = 1.0 / jnp.sqrt((four(deg_col.at[0]) + four(deg_col.at[1]))[0:1])
-        wide[...] = jnp.zeros_like(wide)
-
-        def gram_of(block):
-            wide[0:32, :] = block
-            return dot(block, wide[...], ((1,), (1,)), HIGH)
-
-        for k in range(4):
-            @pl.when(row != 4 * y + k)
-            def _():
-                remote(start_ref, start.at[k], st_send.at[4], st_recv.at[k], sibling).wait_recv()
-        mine = [start[k] for k in range(4)]
-        basis = jnp.concatenate(mine, axis=1)
         inverse = None
         gram_copies = None
         for step in range(6):
@@ -312,58 +352,64 @@
                 basis = dot(inverse, basis, ((1,), (0,)), HIGH)
 
         last[...] = basis
-        last_grams[y] = gram_of(basis)
         owner = lax.div(y, 2) == lax.rem(group, 2)
+
+        def row_copy(k, i, c):
+            return remote(last.at[:, pl.ds((i * 2 + c) * 128, 128)], last_rows, row_send.at[k, i, c],
+                          row_recv.at[0], device(x, lax.rem(y + k, 4), z_hi * 8 + 2 * y + i, c))
+
+        def each_row_copy(do):
+            for k in range(4):
+                for i in (0, 1):
+                    for c in (0, 1):
+                        if k or c:
+                            do(row_copy(k, i, c))
+                        else:
+                            @pl.when(z_lo != 2 * y + i)
+                            def _():
+                                do(row_copy(k, i, c))
+
+        @pl.when(owner)
+        def _():
+            each_row_copy(lambda copy: copy.start())
+            for i in (0, 1):
+                @pl.when(z_lo == 2 * y + i)
+                def _():
+                    last_rows[...] = last[:, i * 256:i * 256 + 128]
+
+        gram = gram_of(basis)
+        last_grams[y] = jnp.concatenate([gram[8 * n:8 * n + 8, :32] for n in range(4)], axis=1)
         waits = []
         for k in range(4):
             for i in range(4):
-                z_to = group * 4 + lax.rem(1 + i, 4)
-                target = device(x, lax.rem(y + k, 4), z_to, core)
-                if k or i:
-                    waits.append(send(last_grams.at[y], last_grams.at[y], fin_send.at[k, i],
-                                      fin_recv.at[y], target))
-
-        def row_copy(k, i):
-            lane = pl.multiple_of((i * 2 + core) * 128, 128)
-            return remote(last.at[:, pl.ds(lane, 128)], last_rows, row_send.at[k, i], row_recv.at[0],
-                          device(x, lax.rem(y + k, 4), z_hi * 8 + 2 * y + i, core))
-
-        for k in range(4):
-            for i in range(2):
-                to_self = (k == 0) & (z_lo == 2 * y + i)
-
-                @pl.when(owner & jnp.logical_not(to_self))
-                def _():
-                    row_copy(k, i).start()
-
-                if k == 0:
-                    @pl.when(owner & to_self)
-                    def _():
-                        lane = pl.multiple_of((i * 2 + core) * 128, 128)
-                        last_rows[...] = last[:, pl.ds(lane, 128)]
+                for c in (0, 1):
+                    if k or i or c:
+                        target = device(x, lax.rem(y + k, 4), group * 4 + lax.rem(1 + i, 4), c)
+                        waits.append(send(last_grams.at[y], last_grams.at[y], fin_send.at[k, i, c],
+                                          fin_recv.at[y], target))
+
         for copy in waits:
             copy.wait_send()
-        for k in range(4):
-            for i in range(2):
-                to_self = (k == 0) & (z_lo == 2 * y + i)
-
-                @pl.when(owner & jnp.logical_not(to_self))
-                def _():
-                    row_copy(k, i).wait_send()
+
+        @pl.when(owner)
+        def _():
+            each_row_copy(lambda copy: copy.wait_send())
 
     for q in range(4):
-        @pl.when(jnp.logical_not(iterates & (y == q)))
-        def _():
-            remote(last_grams.at[q], last_grams.at[q], fin_send.at[0, 0], fin_recv.at[q], sibling).wait_recv()
-    inverse = inverse_factor(four(last_grams))
-
-    @pl.when(jnp.logical_not(iterates & (y == lax.div(z_lo, 2))))
+        @pl.when(jnp.logical_not(iterates & (core == 0) & (y == q)))
+        def _():
+            remote(last_grams.at[q], last_grams.at[q], fin_send.at[0, 0, 0], fin_recv.at[q], sibling).wait_recv()
+    packed = four(last_grams)
+    packed = jnp.concatenate([packed[:, 32 * n:32 * n + 32] for n in range(4)], axis=0)
+    inverse = inverse_factor(jnp.concatenate([packed, jnp.zeros((32, 96), F32)], axis=1))
+
+    @pl.when(jnp.logical_not(iterates & (core == 0) & (y == lax.div(z_lo, 2))))
     def _():
-        remote(last_rows, last_rows, row_send.at[0, 0], row_recv.at[0], sibling).wait_recv()
+        remote(last_rows, last_rows, row_send.at[0, 0, 0], row_recv.at[0], sibling).wait_recv()
 
     out_ref[...] = dot(inverse, last_rows[...], ((1,), (0,)), HIGH) * math.sqrt(SNAPS)
 
-    for n, t in enumerate((2, 3, 10, 11)):
+    for n, t in enumerate((2, 10)):
         @pl.when(giver & (row != t))
         def _():
             basis_copy(n, t).wait_send()
@@ -374,6 +420,7 @@
 
 
 VMEM = pl.BlockSpec(memory_space=pltpu.VMEM)
+ANY = pl.BlockSpec(memory_space=pl.ANY)
 DMA = pltpu.SemaphoreType.DMA
 
 
@@ -381,7 +428,7 @@
     out = pl.pallas_call(
         kernel,
         out_shape=jax.ShapeDtypeStruct((32, 128), F32),
-        in_specs=[VMEM, VMEM],
+        in_specs=[ANY, ANY],
         out_specs=VMEM,
         scratch_shapes=[
             pltpu.VMEM((2, 4, 8, 16, 128), BF16),
@@ -389,11 +436,11 @@
             pltpu.VMEM((2, 4, 8, 4, 16, 128), BF16),
             pltpu.VMEM((2, 4, 4, 16, 512), F32),
             pltpu.VMEM((4, 4, 16, 512), F32),
-            pltpu.VMEM((4, 4, 16, 512), F32),
+            pltpu.VMEM((16, 16, 512), F32),
             pltpu.VMEM((16, 16, 512), F32),
             pltpu.VMEM((16, 512), F32),
             pltpu.VMEM((256, 512), F32),
-            pltpu.VMEM((4, 32, 128), F32),
+            pltpu.VMEM((4, 128, 32), F32),
             pltpu.VMEM((384, 640), F32),
             pltpu.VMEM((512, 512), BF16),
             pltpu.VMEM((512, 512), BF16),
@@ -404,17 +451,17 @@
             pltpu.VMEM((2, 4, 32, 128), F32),
             pltpu.VMEM((32, 512), F32),
             pltpu.VMEM((32, 128), F32),
-            pltpu.VMEM((4, 32, 128), F32),
-            DMA((2, 32)), DMA((2, 32)), DMA((2, 2, 4)), DMA((2, 2, 4)), DMA((2, 2, 4)), DMA((2, 2, 4)),
-            DMA((4,)), DMA((4,)), DMA((1,)), DMA((1,)), DMA((5,)), DMA((1,)), DMA((5,)), DMA((4,)),
-            DMA((3,)), DMA((3,)), DMA((2,)), DMA((2,)), DMA((2, 2, 4)), DMA((2, 2, 4)),
-            DMA((6, 4)), DMA((6, 4)), DMA((2, 4)), DMA((2, 4)), DMA((4, 4)), DMA((4,)),
-            DMA((4, 2)), DMA((1,)),
+            pltpu.VMEM((4, 8, 128), F32),
+            DMA((3,)), DMA((2, 32)), DMA((2, 32)), DMA((2, 2, 4)), DMA((2, 2, 4)), DMA((2, 2, 4)), DMA((2, 2, 4)),
+            DMA((4,)), DMA((4,)), DMA((1,)), DMA((1,)), DMA((5,)), DMA((1,)), DMA((3,)), DMA((4,)),
+            DMA((3,)), DMA((3,)), DMA((2,)), DMA((2,)), DMA((2, 4)), DMA((2, 2, 4)),
+            DMA((6, 4)), DMA((6, 4)), DMA((2, 4)), DMA((2, 4)), DMA((4, 4, 2)), DMA((4,)),
+            DMA((4, 2, 2)), DMA((1,)),
         ],
         compiler_params=pltpu.CompilerParams(
             collective_id=1, has_side_effects=True, vmem_limit_bytes=48 << 20),
         name="subspace",
-    )(snapshots, start_block.T)
+    )(snapshots, start_block)
     return out.T
 
 

time: 146 us -> 146 us (level)
  the two profiles are of different devices: /device:TPU:4 before, /device:TPU:1 now
where the time goes in v3:
time: 146 us
  Pallas kernels  144 us (99%)
  local copies, waits for them, and re-layouts  2.37 us (2%)
    pallas_call x1, Pallas kernels, body(): pl.pallas_call(kernel, out_shape=jax.ShapeDtypeStruct((32, 128), F32), in...  144 us

profile of v3, /device:TPU:1, one launch (start us, length us, event | category | flops | bytes accessed | tf_op | source)
XLA Modules:
  0.0 146.2 jit_solution(15629876831620099450)
XLA Ops:
  0.0 0.8 copy.3.start_ref
  0.8 0.0 copy-start
  0.8 0.9 copy-done
  1.8 143.8 %subspace.1 = f32[32,128]{1,0:T(8,128)S(1)} custom-call(bf16[16,8192]{1,0:T(8,128)(2,1)S(1)} %copy-done, f32[128,32]{1,0:T(8,128)S(1)} %copy.3.start_ref), custom_call_target="tpu_custom_call" | custom-call | tf_op jit(solution)/shard_map/subspace/pallas_call | solution.py:428
  145.6 0.6 copy.5
Async XLA Ops:
  0.8 1.0 copy-start

commit v4 on v3

--- a/solution.py
+++ b/solution.py
@@ -32,6 +32,14 @@
     copy = remote(*args)
     copy.start()
     return copy
+
+
+def send_pieces(count, src, dst, send_sem, recv_sem, target):
+    rows = src.shape[0] // count
+    for n in range(count):
+        piece = pl.ds(n * rows, rows)
+        send(src.at[piece], dst.at[piece], send_sem, recv_sem, target)
+    return remote(src, dst, send_sem, recv_sem, target)
 
 
 def dot(a, b, dims, precision=None):
@@ -73,11 +81,11 @@
 
 def kernel(
     x_ref, start_ref, out_ref,
-    zbuf, abuf, bbuf, part, sib, own, rsbuf, total, dist, start,
+    zbuf, abuf, bbuf, part, sib, own, rs_up, rs_down, rs_near, rs_sum, rs_last, total, start,
     ext, kern_hi, kern_lo, deg_row, deg_col, wide, income, grams, last, last_rows, last_grams,
     local_sem, z_send, z_recv, plane_send, plane_recv, gather_send, gather_recv,
     sib_send, sib_recv, rs_send, rs_recv, ag_send, ag_recv, st_send, st_recv,
-    halo_send, halo_recv, core_send, core_recv, deg_send, deg_recv,
+    core_send, core_recv, deg_send, deg_recv,
     step_send, step_recv, gram_send, gram_recv, fin_send, fin_recv, row_send, row_recv,
 ):
     row, col, y = lax.axis_index("row"), lax.axis_index("col"), lax.axis_index("feat")
@@ -167,12 +175,12 @@
         for copy, _ in first[h]:
             copy.wait()
         for k in (1, 2, 3):
-            group_copies.append(send(abuf.at[h, y], abuf.at[h, y],
+            group_copies.append(send_pieces(4, abuf.at[h, y], abuf.at[h, y],
                                      gather_send.at[h, 0, k], gather_recv.at[h, 0, k], along_y(k)))
         for _, copy in first[h]:
             copy.wait()
         for k in (1, 2, 3):
-            group_copies.append(send(bbuf.at[h, :, :, x], bbuf.at[h, :, :, x],
+            group_copies.append(send_pieces(4, bbuf.at[h, :, :, x], bbuf.at[h, :, :, x],
                                      gather_send.at[h, 1, k], gather_recv.at[h, 1, k], along_x(k)))
         gathers.append(group_copies)
 
@@ -193,50 +201,74 @@
                 value = value + part[half]
             part[half] = value
             if h == 1 and half is not core:
-                core_sums = [send(part.at[half, n], sib.at[n], sib_send.at[n], sib_recv.at[n], sibling)
+                core_sums = [send_pieces(2, part.at[half, n], sib.at[n], sib_send.at[n], sib_recv.at[n], sibling)
                              for n in range(4)]
 
     for n in range(4):
         core_sums[n].wait()
         own[pl.ds(n * 4, 4)] = part[core, n] + sib[n]
-    for o in sorted(range(1, 16), key=lambda o: -min(o, 16 - o)):
-        q = lax.rem(z + o, 16)
-        send(own.at[q], rsbuf.at[z], rs_send.at[0], rs_recv.at[0], device(x, y, q, core))
-    rsbuf[z] = own[z]
-    remote(rsbuf.at[pl.ds(0, 15)], rsbuf.at[pl.ds(0, 15)], rs_send.at[0], rs_recv.at[0], sibling).wait()
-    chunk = rsbuf[0]
-    for q in range(1, 16):
-        chunk = chunk + rsbuf[q]
-    total[...] = chunk
-
-    my_rows = pl.ds(pl.multiple_of(z * 16, 16), 16)
-
-    def gather(n, p):
-        return remote(total, dist.at[my_rows, :], ag_send.at[n], ag_recv.at[0], device(x, y, p, core))
-
-    for n, p in enumerate(PLANES):
-        @pl.when(z != p)
-        def _():
-            gather(n, p).start()
+
+    def at_plane(o):
+        return device(x, y, lax.rem(z + o + 16, 16), core)
+
+    for d in (8, 7, 6, 5):
+        send(own.at[lax.rem(z + d, 16)], rs_up.at[d - 5], rs_send.at[0], rs_recv.at[0], at_plane(d - 4))
+        if d < 8:
+            send(own.at[lax.rem(z + 16 - d, 16)], rs_down.at[d - 5], rs_send.at[1], rs_recv.at[1], at_plane(4 - d))
+    for d in (3, 2, 1):
+        send(own.at[lax.rem(z + d, 16)], rs_near.at[d - 1], rs_send.at[2], rs_recv.at[2], at_plane(d))
+        send(own.at[lax.rem(z + 16 - d, 16)], rs_near.at[d + 2], rs_send.at[2], rs_recv.at[2], at_plane(-d))
+    remote(rs_up, rs_up, rs_send.at[0], rs_recv.at[0], sibling).wait_recv()
+    rs_sum[0] = own[lax.rem(z + 4, 16)] + four(rs_up)
+    last_up = send(rs_sum.at[0], rs_last.at[0], rs_send.at[3], rs_recv.at[3], at_plane(4))
+    remote(rs_down, rs_down, rs_send.at[1], rs_recv.at[1], sibling).wait_recv()
+    rs_sum[1] = own[lax.rem(z + 12, 16)] + (rs_down[0] + rs_down[1] + rs_down[2])
+    last_down = send(rs_sum.at[1], rs_last.at[1], rs_send.at[4], rs_recv.at[4], at_plane(-4))
+    remote(rs_near, rs_near, rs_send.at[2], rs_recv.at[2], sibling).wait()
+    near = own[z] + ((rs_near[0] + rs_near[1]) + (rs_near[2] + rs_near[3]) + (rs_near[4] + rs_near[5]))
+    last_up.wait()
+    last_down.wait()
+    total[...] = near + (rs_last[0] + rs_last[1])
+    remote(rs_up, rs_up, rs_send.at[0], rs_recv.at[0], sibling).wait_send()
+    remote(rs_down, rs_down, rs_send.at[1], rs_recv.at[1], sibling).wait_send()
+
+    x_next, y_next = lax.rem(x + core, 4), lax.rem(y + 1, 4)
+
+    def strip(first):
+        return pl.ds(pl.multiple_of(first, 16), 16)
+
+    def gather(n, p, part_at):
+        below, right = part_at
+        edge = total.at[:, pl.ds(384, 128)] if right else total
+        lanes = pl.ds(0, 128) if right else pl.ds(128, 512)
+        rows = strip(jnp.maximum(z - 8, 0) * 16) if below else strip(128 + z * 16)
+        return remote(edge, ext.at[rows, lanes], ag_send.at[n, below, right], ag_recv.at[below, right],
+                      device(x_next if below else x, y_next if right else y, p,
+                             1 - core if below else core))
+
+    def each_gather(do):
+        for n, p in enumerate(PLANES):
+            @pl.when(z != p)
+            def _():
+                do(gather(n, p, (0, 0)))
+
+            @pl.when(z >= 8)
+            def _():
+                do(gather(n, p, (1, 0)))
+                do(gather(n, p, (1, 1)))
+
+            do(gather(n, p, (0, 1)))
+
+    each_gather(lambda copy: copy.start())
 
     @pl.when(iterates)
     def _():
-        dist[my_rows, :] = total[...]
-        remote(dist.at[pl.ds(0, 240), :], dist.at[pl.ds(0, 240), :],
-               ag_send.at[4], ag_recv.at[0], sibling).wait_recv()
-
-        x_next, y_next = lax.rem(x + core, 4), lax.rem(y + 1, 4)
-        halo = [
-            send(dist.at[pl.ds(128, 128), :], ext.at[pl.ds(0, 128), pl.ds(128, 512)],
-                 halo_send.at[0], halo_recv.at[0], device(x_next, y, z, 1 - core)),
-            send(dist.at[:, pl.ds(384, 128)], ext.at[pl.ds(128, 256), pl.ds(0, 128)],
-                 halo_send.at[1], halo_recv.at[1], device(x, y_next, z, core)),
-            send(dist.at[pl.ds(128, 128), pl.ds(384, 128)], ext.at[pl.ds(0, 128), pl.ds(0, 128)],
-                 halo_send.at[2], halo_recv.at[2], device(x_next, y_next, z, 1 - core)),
-        ]
-        ext[128:384, 128:640] = dist[...]
-        for copy in halo:
-            copy.wait()
+        ext[strip(128 + z * 16), 128:640] = total[...]
+        for n, (rows, lanes) in enumerate((
+                (pl.ds(0, 240), pl.ds(128, 512)), (pl.ds(128, 256), pl.ds(0, 128)),
+                (pl.ds(0, 128), pl.ds(128, 512)), (pl.ds(0, 128), pl.ds(0, 128)))):
+            view = ext.at[rows, lanes]
+            remote(view, view, ag_send.at[0, 0, 0], ag_recv.at[n // 2, n % 2], sibling).wait_recv()
         rows = lax.broadcasted_iota(jnp.int32, (384, 640), 0)
         lanes = lax.broadcasted_iota(jnp.int32, (384, 640), 1)
         first_row = jnp.where(2 * x + core == 0, 128, 0)
@@ -264,8 +296,8 @@
 
         @pl.when(core == 1)
         def _():
-            for copy in swaps:
-                copy.start()
+            for n, ref in enumerate((kern_hi, kern_lo)):
+                send_pieces(4, ref.at[my_half, :], ref.at[my_half, :], core_send.at[n], core_recv.at[n], sibling)
 
         ones = jnp.ones((8, 512), F32)
         deg_row[core, y] = dot(ones, half_tile, ((1,), (1,)), HIGH)
@@ -334,7 +366,7 @@
             copies = []
             for k in (1, 2, 3):
                 view = income.at[step, at]
-                copies.append(send(view, view, step_send.at[step, k], step_recv.at[step, k],
+                copies.append(send_pieces(2, view, view, step_send.at[step, k], step_recv.at[step, k],
                                    along_y(k) if over_y else along_x(k)))
             if step in (2, 4):
                 n = step // 2 - 1
@@ -351,7 +383,6 @@
             if step in (3, 5):
                 basis = dot(inverse, basis, ((1,), (0,)), HIGH)
 
-        last[...] = basis
         owner = lax.div(y, 2) == lax.rem(group, 2)
 
         def row_copy(k, i, c):
@@ -369,14 +400,6 @@
                             def _():
                                 do(row_copy(k, i, c))
 
-        @pl.when(owner)
-        def _():
-            each_row_copy(lambda copy: copy.start())
-            for i in (0, 1):
-                @pl.when(z_lo == 2 * y + i)
-                def _():
-                    last_rows[...] = last[:, i * 256:i * 256 + 128]
-
         gram = gram_of(basis)
         last_grams[y] = jnp.concatenate([gram[8 * n:8 * n + 8, :32] for n in range(4)], axis=1)
         waits = []
@@ -388,6 +411,16 @@
                         waits.append(send(last_grams.at[y], last_grams.at[y], fin_send.at[k, i, c],
                                           fin_recv.at[y], target))
 
+        last[...] = basis
+
+        @pl.when(owner)
+        def _():
+            each_row_copy(lambda copy: copy.start())
+            for i in (0, 1):
+                @pl.when(z_lo == 2 * y + i)
+                def _():
+                    last_rows[...] = last[:, i * 256:i * 256 + 128]
+
         for copy in waits:
             copy.wait_send()
 
@@ -413,10 +446,7 @@
         @pl.when(giver & (row != t))
         def _():
             basis_copy(n, t).wait_send()
-    for n, p in enumerate(PLANES):
-        @pl.when(z != p)
-        def _():
-            gather(n, p).wait_send()
+    each_gather(lambda copy: copy.wait_send())
 
 
 VMEM = pl.BlockSpec(memory_space=pltpu.VMEM)
@@ -437,9 +467,12 @@
             pltpu.VMEM((2, 4, 4, 16, 512), F32),
             pltpu.VMEM((4, 4, 16, 512), F32),
             pltpu.VMEM((16, 16, 512), F32),
-            pltpu.VMEM((16, 16, 512), F32),
+            pltpu.VMEM((4, 16, 512), F32),
+            pltpu.VMEM((3, 16, 512), F32),
+            pltpu.VMEM((6, 16, 512), F32),
+            pltpu.VMEM((2, 16, 512), F32),
+            pltpu.VMEM((2, 16, 512), F32),
             pltpu.VMEM((16, 512), F32),
-            pltpu.VMEM((256, 512), F32),
             pltpu.VMEM((4, 128, 32), F32),
             pltpu.VMEM((384, 640), F32),
             pltpu.VMEM((512, 512), BF16),
@@ -453,8 +486,8 @@
             pltpu.VMEM((32, 128), F32),
             pltpu.VMEM((4, 8, 128), F32),
             DMA((3,)), DMA((2, 32)), DMA((2, 32)), DMA((2, 2, 4)), DMA((2, 2, 4)), DMA((2, 2, 4)), DMA((2, 2, 4)),
-            DMA((4,)), DMA((4,)), DMA((1,)), DMA((1,)), DMA((5,)), DMA((1,)), DMA((3,)), DMA((4,)),
-            DMA((3,)), DMA((3,)), DMA((2,)), DMA((2,)), DMA((2, 4)), DMA((2, 2, 4)),
+            DMA((4,)), DMA((4,)), DMA((5,)), DMA((5,)), DMA((4, 2, 2)), DMA((2, 2)), DMA((3,)), DMA((4,)),
+            DMA((2,)), DMA((2,)), DMA((2, 4)), DMA((2, 2, 4)),
             DMA((6, 4)), DMA((6, 4)), DMA((2, 4)), DMA((2, 4)), DMA((4, 4, 2)), DMA((4,)),
             DMA((4, 2, 2)), DMA((1,)),
         ],

time: 146 us -> 139 us (0.952)
  Pallas kernels: 144 us -> 136 us
    pallas_call x1, Pallas kernels: 144 us -> 136 us  [body(): pl.pallas_call(kernel, out_shape=jax.ShapeDtypeStruct((32, 128), F32), in...]
where the time goes in v4:
time: 139 us
  Pallas kernels  136 us (98%)
  local copies, waits for them, and re-layouts  2.37 us (2%)
    pallas_call x1, Pallas kernels, body(): pl.pallas_call(kernel, out_shape=jax.ShapeDtypeStruct((32, 128), F32), in...  136 us

profile of v4, /device:TPU:1, one launch (start us, length us, event | category | flops | bytes accessed | tf_op | source)
XLA Modules:
  0.0 138.9 jit_solution(9670022796941272306)
XLA Ops:
  0.0 0.8 copy.3.start_ref
  0.8 0.0 copy-start
  0.8 0.9 copy-done
  1.8 136.5 %subspace.1 = f32[32,128]{1,0:T(8,128)S(1)} custom-call(bf16[16,8192]{1,0:T(8,128)(2,1)S(1)} %copy-done, f32[128,32]{1,0:T(8,128)S(1)} %copy.3.start_ref), custom_call_target="tpu_custom_call" | custom-call | tf_op jit(solution)/shard_map/subspace/pallas_call | solution.py:458
  138.3 0.6 copy.5
Async XLA Ops:
  0.8 1.0 copy-start

commit v5 on v4

--- a/solution.py
+++ b/solution.py
@@ -85,7 +85,7 @@
     ext, kern_hi, kern_lo, deg_row, deg_col, wide, income, grams, last, last_rows, last_grams,
     local_sem, z_send, z_recv, plane_send, plane_recv, gather_send, gather_recv,
     sib_send, sib_recv, rs_send, rs_recv, ag_send, ag_recv, st_send, st_recv,
-    core_send, core_recv, deg_send, deg_recv,
+    halo_send, halo_recv, core_send, core_recv, deg_send, deg_recv,
     step_send, step_recv, gram_send, gram_recv, fin_send, fin_recv, row_send, row_recv,
 ):
     row, col, y = lax.axis_index("row"), lax.axis_index("col"), lax.axis_index("feat")
@@ -232,43 +232,40 @@
     remote(rs_up, rs_up, rs_send.at[0], rs_recv.at[0], sibling).wait_send()
     remote(rs_down, rs_down, rs_send.at[1], rs_recv.at[1], sibling).wait_send()
 
-    x_next, y_next = lax.rem(x + core, 4), lax.rem(y + 1, 4)
-
-    def strip(first):
-        return pl.ds(pl.multiple_of(first, 16), 16)
-
-    def gather(n, p, part_at):
-        below, right = part_at
-        edge = total.at[:, pl.ds(384, 128)] if right else total
-        lanes = pl.ds(0, 128) if right else pl.ds(128, 512)
-        rows = strip(jnp.maximum(z - 8, 0) * 16) if below else strip(128 + z * 16)
-        return remote(edge, ext.at[rows, lanes], ag_send.at[n, below, right], ag_recv.at[below, right],
-                      device(x_next if below else x, y_next if right else y, p,
-                             1 - core if below else core))
+    my_rows = pl.ds(pl.multiple_of(128 + z * 16, 16), 16)
+
+    def gather(n, p):
+        return remote(total, ext.at[my_rows, pl.ds(128, 512)], ag_send.at[n], ag_recv.at[0],
+                      device(x, y, p, core))
 
     def each_gather(do):
         for n, p in enumerate(PLANES):
             @pl.when(z != p)
             def _():
-                do(gather(n, p, (0, 0)))
-
-            @pl.when(z >= 8)
-            def _():
-                do(gather(n, p, (1, 0)))
-                do(gather(n, p, (1, 1)))
-
-            do(gather(n, p, (0, 1)))
+                do(gather(n, p))
 
     each_gather(lambda copy: copy.start())
 
     @pl.when(iterates)
     def _():
-        ext[strip(128 + z * 16), 128:640] = total[...]
-        for n, (rows, lanes) in enumerate((
-                (pl.ds(0, 240), pl.ds(128, 512)), (pl.ds(128, 256), pl.ds(0, 128)),
-                (pl.ds(0, 128), pl.ds(128, 512)), (pl.ds(0, 128), pl.ds(0, 128)))):
-            view = ext.at[rows, lanes]
-            remote(view, view, ag_send.at[0, 0, 0], ag_recv.at[n // 2, n % 2], sibling).wait_recv()
+        ext[my_rows, 128:640] = total[...]
+        view = ext.at[pl.ds(0, 240), pl.ds(128, 512)]
+        remote(view, view, ag_send.at[0], ag_recv.at[0], sibling).wait_recv()
+
+        x_next, y_next = lax.rem(x + core, 4), lax.rem(y + 1, 4)
+        below, right, both = (
+            device(x_next, y, z, 1 - core), device(x, y_next, z, core), device(x_next, y_next, z, 1 - core))
+        bottom, inner, edge = pl.ds(256, 128), pl.ds(128, 512), pl.ds(512, 128)
+        halo = [
+            send_pieces(4, ext.at[bottom, inner], ext.at[pl.ds(0, 128), inner],
+                        halo_send.at[0], halo_recv.at[0], below),
+            send_pieces(2, ext.at[bottom, edge], ext.at[pl.ds(0, 128), pl.ds(0, 128)],
+                        halo_send.at[2], halo_recv.at[2], both),
+            send_pieces(4, ext.at[pl.ds(128, 256), edge], ext.at[pl.ds(128, 256), pl.ds(0, 128)],
+                        halo_send.at[1], halo_recv.at[1], right),
+        ]
+        for copy in halo:
+            copy.wait()
         rows = lax.broadcasted_iota(jnp.int32, (384, 640), 0)
         lanes = lax.broadcasted_iota(jnp.int32, (384, 640), 1)
         first_row = jnp.where(2 * x + core == 0, 128, 0)
@@ -299,9 +296,10 @@
             for n, ref in enumerate((kern_hi, kern_lo)):
                 send_pieces(4, ref.at[my_half, :], ref.at[my_half, :], core_send.at[n], core_recv.at[n], sibling)
 
-        ones = jnp.ones((8, 512), F32)
-        deg_row[core, y] = dot(ones, half_tile, ((1,), (1,)), HIGH)
-        deg_col[core, x] = dot(ones[:, :256], half_tile, ((1,), (0,)), HIGH)
+        ones = jnp.ones((16, 512), BF16)
+        deg_row[core, y] = (dot(ones, half_hi, ((1,), (1,))) + dot(ones, half_lo, ((1,), (1,))))[:8]
+        deg_col[core, x] = (dot(ones[:, :256], half_hi, ((1,), (0,)))
+                            + dot(ones[:, :256], half_lo, ((1,), (0,))))[:8]
 
         def degree_copies(k):
             row_view, col_view = deg_row.at[core, y], deg_col.at[core, x]
@@ -486,8 +484,8 @@
             pltpu.VMEM((32, 128), F32),
             pltpu.VMEM((4, 8, 128), F32),
             DMA((3,)), DMA((2, 32)), DMA((2, 32)), DMA((2, 2, 4)), DMA((2, 2, 4)), DMA((2, 2, 4)), DMA((2, 2, 4)),
-            DMA((4,)), DMA((4,)), DMA((5,)), DMA((5,)), DMA((4, 2, 2)), DMA((2, 2)), DMA((3,)), DMA((4,)),
-            DMA((2,)), DMA((2,)), DMA((2, 4)), DMA((2, 2, 4)),
+            DMA((4,)), DMA((4,)), DMA((5,)), DMA((5,)), DMA((4,)), DMA((1,)), DMA((3,)), DMA((4,)),
+            DMA((3,)), DMA((3,)), DMA((2,)), DMA((2,)), DMA((2, 4)), DMA((2, 2, 4)),
             DMA((6, 4)), DMA((6, 4)), DMA((2, 4)), DMA((2, 4)), DMA((4, 4, 2)), DMA((4,)),
             DMA((4, 2, 2)), DMA((1,)),
         ],

time: 139 us -> 136 us (0.978)
  Pallas kernels: 136 us -> 133 us
    pallas_call x1, Pallas kernels: 136 us -> 133 us  [body(): pl.pallas_call(kernel, out_shape=jax.ShapeDtypeStruct((32, 128), F32), in...]
where the time goes in v5:
time: 136 us
  Pallas kernels  133 us (98%)
  local copies, waits for them, and re-layouts  2.37 us (2%)
    pallas_call x1, Pallas kernels, body(): pl.pallas_call(kernel, out_shape=jax.ShapeDtypeStruct((32, 128), F32), in...  133 us

profile of v5, /device:TPU:1, one launch (start us, length us, event | category | flops | bytes accessed | tf_op | source)
XLA Modules:
  0.0 135.9 jit_solution(3021581350776166945)
XLA Ops:
  0.0 0.8 copy.3.start_ref
  0.8 0.0 copy-start
  0.8 0.9 copy-done
  1.8 133.5 %subspace.1 = f32[32,128]{1,0:T(8,128)S(1)} custom-call(bf16[16,8192]{1,0:T(8,128)(2,1)S(1)} %copy-done, f32[128,32]{1,0:T(8,128)S(1)} %copy.3.start_ref), custom_call_target="tpu_custom_call" | custom-call | tf_op jit(solution)/shard_map/subspace/pallas_call | solution.py:456
  135.3 0.6 copy.5
Async XLA Ops:
  0.8 1.0 copy-start

commit v6 on v5

--- a/solution.py
+++ b/solution.py
@@ -160,7 +160,7 @@
                 copy.wait_send()
             copy.wait_recv()
         pairs = []
-        for k in (1, 2, 3):
+        for k in (2, 1, 3):
             pairs.append((
                 send(zbuf.at[h, lax.rem(x + k, 4)], abuf.at[h, y, :, x],
                      plane_send.at[h, 0, k], plane_recv.at[h, 0, k], along_x(k)),
@@ -174,12 +174,12 @@
         group_copies = []
         for copy, _ in first[h]:
             copy.wait()
-        for k in (1, 2, 3):
+        for k in (2, 1, 3):
             group_copies.append(send_pieces(4, abuf.at[h, y], abuf.at[h, y],
                                      gather_send.at[h, 0, k], gather_recv.at[h, 0, k], along_y(k)))
         for _, copy in first[h]:
             copy.wait()
-        for k in (1, 2, 3):
+        for k in (2, 1, 3):
             group_copies.append(send_pieces(4, bbuf.at[h, :, :, x], bbuf.at[h, :, :, x],
                                      gather_send.at[h, 1, k], gather_recv.at[h, 1, k], along_x(k)))
         gathers.append(group_copies)
@@ -308,7 +308,7 @@
 
         @pl.when(core == 1)
         def _():
-            for k in range(4):
+            for k in (2, 1, 3, 0):
                 for copy in degree_copies(k):
                     copy.start()
             for copy in swaps:
@@ -323,7 +323,7 @@
             ref = (deg_row, deg_col)[n].at[c, 0]
             return remote(ref, ref, deg_send.at[n, k], deg_recv.at[n, c, k], sibling)
 
-        for k in (1, 2, 3):
+        for k in (2, 1, 3):
             for n, ref, target in ((0, deg_row.at[0, y], along_y(k)), (1, deg_col.at[0, x], along_x(k))):
                 remote(ref, ref, deg_send.at[n, k], deg_recv.at[n, 0, k], target).start()
         wide[...] = jnp.zeros_like(wide)
@@ -337,11 +337,10 @@
             def _():
                 remote(start_ref, start.at[k], st_send.at[2], st_recv.at[k], sibling).wait_recv()
         mine = [start[k].T for k in range(4)]
-        basis = jnp.concatenate(mine, axis=1)
+        basis = [jnp.concatenate(mine[:2], axis=1), jnp.concatenate(mine[2:], axis=1)]
         other_half = pl.ds(256, 256)
         for n, ref in enumerate((kern_hi, kern_lo)):
             remote(ref.at[other_half, :], ref.at[other_half, :], core_send.at[n], core_recv.at[n], sibling).wait_recv()
-        tile_hi, tile_lo = kern_hi[...], kern_lo[...]
         for n in (0, 1):
             for k in (1, 2, 3):
                 degree_copy(n, 0, k).wait()
@@ -350,36 +349,54 @@
         row_sums = jnp.concatenate([four(deg_row.at[0]), four(deg_row.at[1])], axis=1)[0:1]
         scale_row = 1.0 / jnp.sqrt(row_sums)
         scale_col = 1.0 / jnp.sqrt((four(deg_col.at[0]) + four(deg_col.at[1]))[0:1])
+        scale_row = scale_row[:, :256], scale_row[:, 256:]
+        scale_col = scale_col[:, :256], scale_col[:, 256:]
+
+        def term(over_y, n, m, block):
+            n, m = pl.ds(n * 256, 256), pl.ds(m * 256, 256)
+            at, dims = ((m, n), ((1,), (1,))) if over_y else ((n, m), ((1,), (0,)))
+            high = dot(jnp.concatenate(block, axis=0), kern_hi[at], dims)
+            low = dot(jnp.concatenate(block[:2], axis=0), kern_lo[at], dims)
+            return high[:32] + ((high[32:64] + low[:32]) + (high[64:] + low[32:]))
+
+        def arrived(step, n):
+            for copy in copies[n]:
+                copy.wait()
+            block = four(income.at[step, n])
+            return dot(inverse, block, ((1,), (0,)), HIGH) if step in (3, 5) else block
+
         inverse = None
         gram_copies = None
+        copies = None
         for step in range(6):
             over_y = step % 2 == 0
             at = y if over_y else x
-            scaled = parts(basis * (scale_col if over_y else scale_row), 3)
-            dims = ((1,), (1,)) if over_y else ((1,), (0,))
-            high = dot(jnp.concatenate(scaled, axis=0), tile_hi, dims)
-            low = dot(jnp.concatenate(scaled[:2], axis=0), tile_lo, dims)
-            product = high[:32] + ((high[32:64] + low[:32]) + (high[64:] + low[32:]))
-            income[step, at] = product * (scale_row if over_y else scale_col)
-            copies = []
-            for k in (1, 2, 3):
-                view = income.at[step, at]
-                copies.append(send_pieces(2, view, view, step_send.at[step, k], step_recv.at[step, k],
-                                   along_y(k) if over_y else along_x(k)))
+            scale_in, scale_out = (scale_col, scale_row) if over_y else (scale_row, scale_col)
+            sums = None
+            sent = []
+            for n in (0, 1):
+                if step:
+                    basis[n] = arrived(step - 1, n)
+                block = parts(basis[n] * scale_in[n], 3)
+                if n == 0:
+                    sums = [term(over_y, 0, m, block) for m in (0, 1)]
+                    continue
+                for m in (0, 1):
+                    income[step, m, at] = (sums[m] + term(over_y, 1, m, block)) * scale_out[m]
+                    view = income.at[step, m, at]
+                    sent.append([send(view, view, step_send.at[step, m, k], step_recv.at[step, m, k],
+                                      along_y(k) if over_y else along_x(k)) for k in (2, 1, 3)])
+            copies = sent
             if step in (2, 4):
                 n = step // 2 - 1
-                grams[n, y] = gram_of(basis)
+                grams[n, y] = gram_of(jnp.concatenate(basis, axis=1))
                 gram_copies = [send(grams.at[n, y], grams.at[n, y], gram_send.at[n, k],
-                                    gram_recv.at[n, k], along_y(k)) for k in (1, 2, 3)]
+                                    gram_recv.at[n, k], along_y(k)) for k in (2, 1, 3)]
             if step in (3, 5):
                 for copy in gram_copies:
                     copy.wait()
                 inverse = inverse_factor(four(grams.at[step // 2 - 1]))
-            for copy in copies:
-                copy.wait()
-            basis = four(income.at[step])
-            if step in (3, 5):
-                basis = dot(inverse, basis, ((1,), (0,)), HIGH)
+        basis = jnp.concatenate([arrived(5, 0), arrived(5, 1)], axis=1)
 
         owner = lax.div(y, 2) == lax.rem(group, 2)
 
@@ -388,7 +405,7 @@
                           row_recv.at[0], device(x, lax.rem(y + k, 4), z_hi * 8 + 2 * y + i, c))
 
         def each_row_copy(do):
-            for k in range(4):
+            for k in (2, 1, 3, 0):
                 for i in (0, 1):
                     for c in (0, 1):
                         if k or c:
@@ -401,8 +418,8 @@
         gram = gram_of(basis)
         last_grams[y] = jnp.concatenate([gram[8 * n:8 * n + 8, :32] for n in range(4)], axis=1)
         waits = []
-        for k in range(4):
-            for i in range(4):
+        for k in (2, 1, 3, 0):
+            for i in (2, 1, 3, 0):
                 for c in (0, 1):
                     if k or i or c:
                         target = device(x, lax.rem(y + k, 4), group * 4 + lax.rem(1 + i, 4), c)
@@ -478,7 +495,7 @@
             pltpu.VMEM((2, 4, 8, 256), F32),
             pltpu.VMEM((2, 4, 8, 512), F32),
             pltpu.VMEM((128, 512), F32),
-            pltpu.VMEM((6, 4, 32, 512), F32),
+            pltpu.VMEM((6, 2, 4, 32, 256), F32),
             pltpu.VMEM((2, 4, 32, 128), F32),
             pltpu.VMEM((32, 512), F32),
             pltpu.VMEM((32, 128), F32),
@@ -486,7 +503,7 @@
             DMA((3,)), DMA((2, 32)), DMA((2, 32)), DMA((2, 2, 4)), DMA((2, 2, 4)), DMA((2, 2, 4)), DMA((2, 2, 4)),
             DMA((4,)), DMA((4,)), DMA((5,)), DMA((5,)), DMA((4,)), DMA((1,)), DMA((3,)), DMA((4,)),
             DMA((3,)), DMA((3,)), DMA((2,)), DMA((2,)), DMA((2, 4)), DMA((2, 2, 4)),
-            DMA((6, 4)), DMA((6, 4)), DMA((2, 4)), DMA((2, 4)), DMA((4, 4, 2)), DMA((4,)),
+            DMA((6, 2, 4)), DMA((6, 2, 4)), DMA((2, 4)), DMA((2, 4)), DMA((4, 4, 2)), DMA((4,)),
             DMA((4, 2, 2)), DMA((1,)),
         ],
         compiler_params=pltpu.CompilerParams(

time: 136 us -> 134 us (0.985)
  Pallas kernels: 133 us -> 131 us
    pallas_call x1, Pallas kernels: 133 us -> 131 us  [body(): pl.pallas_call(kernel, out_shape=jax.ShapeDtypeStruct((32, 128), F32), in...]
where the time goes in v6:
time: 134 us
  Pallas kernels  131 us (98%)
  local copies, waits for them, and re-layouts  2.37 us (2%)
    pallas_call x1, Pallas kernels, body(): pl.pallas_call(kernel, out_shape=jax.ShapeDtypeStruct((32, 128), F32), in...  131 us

profile of v6, /device:TPU:1, one launch (start us, length us, event | category | flops | bytes accessed | tf_op | source)
XLA Modules:
  0.0 133.8 jit_solution(8321285361531171831)
XLA Ops:
  0.0 0.8 copy.3.start_ref
  0.8 0.0 copy-start
  0.8 0.9 copy-done
  1.8 131.5 %subspace.1 = f32[32,128]{1,0:T(8,128)S(1)} custom-call(bf16[16,8192]{1,0:T(8,128)(2,1)S(1)} %copy-done, f32[128,32]{1,0:T(8,128)S(1)} %copy.3.start_ref), custom_call_target="tpu_custom_call" | custom-call | tf_op jit(solution)/shard_map/subspace/pallas_call | solution.py:473
  133.2 0.6 copy.5
Async XLA Ops:
  0.8 1.0 copy-start

commit v7 on v6

--- a/solution.py
+++ b/solution.py
@@ -10,7 +10,6 @@
 PTS = 32768
 LAGS = 128
 SNAPS = 2048
-PLANES = (1, 5, 9, 13)
 MESH = pl.DeviceIdType.MESH
 HIGH = lax.Precision.HIGHEST
 F32 = jnp.float32
@@ -60,17 +59,16 @@
     rows = lax.broadcasted_iota(jnp.int32, (32, 128), 0)
     lanes = lax.broadcasted_iota(jnp.int32, (32, 128), 1)
     work = jnp.where(lanes < 32, gram, jnp.where(lanes - 32 == rows, 1.0, 0.0))
-    for k in range(0, 32, 2):
-        top, next_top = work[k:k + 1, :], work[k + 1:k + 2, :]
-        left, right = work[:, k:k + 1], work[:, k + 1:k + 2]
-        scale = 1.0 / top[:, k:k + 1]
-        ratio = left * scale
-        step = next_top[:, k:k + 1] * scale
-        next_top = next_top - step * top
-        next_ratio = (right - ratio * top[:, k + 1:k + 2]) / next_top[:, k + 1:k + 2]
-        first = jnp.where(rows > k, ratio, 0.0)
-        second = jnp.where(rows > k + 1, next_ratio, 0.0)
-        work = (work - first * top) - second * next_top
+    for k in range(0, 32, 16):
+        tops = [work[k + n:k + n + 1, :] for n in range(16)]
+        columns = [jnp.broadcast_to(work[:, k + n:k + n + 1], (32, 128)) for n in range(16)]
+        for n in range(16):
+            at = k + n
+            ratio = columns[n] * (1.0 / columns[n][at:at + 1, :])
+            for m in range(n + 1, 16):
+                tops[m] = tops[m] - ratio[k + m:k + m + 1, :] * tops[n]
+                columns[m] = columns[m] - ratio * columns[m][at:at + 1, :]
+            work = work - jnp.where(rows > at, ratio, 0.0) * tops[n]
     diagonal = jnp.sum(jnp.where(lanes == rows, work, 0.0), axis=1, keepdims=True)
     return work[:, 32:64] / jnp.sqrt(diagonal)
 
@@ -235,16 +233,18 @@
     my_rows = pl.ds(pl.multiple_of(128 + z * 16, 16), 16)
 
     def gather(n, p):
-        return remote(total, ext.at[my_rows, pl.ds(128, 512)], ag_send.at[n], ag_recv.at[0],
-                      device(x, y, p, core))
+        return (total, ext.at[my_rows, pl.ds(128, 512)], ag_send.at[n], ag_recv.at[0],
+                device(x, y, p, core))
 
     def each_gather(do):
-        for n, p in enumerate(PLANES):
-            @pl.when(z != p)
-            def _():
-                do(gather(n, p))
-
-    each_gather(lambda copy: copy.start())
+        for n in (2, 1, 3):
+            do(gather(n, lax.rem(group + n, 4) * 4 + 1))
+
+        @pl.when(jnp.logical_not(iterates))
+        def _():
+            do(gather(0, group * 4 + 1))
+
+    each_gather(lambda copy: send_pieces(2, *copy))
 
     @pl.when(iterates)
     def _():
@@ -461,7 +461,7 @@
         @pl.when(giver & (row != t))
         def _():
             basis_copy(n, t).wait_send()
-    each_gather(lambda copy: copy.wait_send())
+    each_gather(lambda copy: remote(*copy).wait_send())
 
 
 VMEM = pl.BlockSpec(memory_space=pltpu.VMEM)

time: 134 us -> 132 us (0.985)
  Pallas kernels: 131 us -> 129 us
    pallas_call x1, Pallas kernels: 131 us -> 129 us  [body(): pl.pallas_call(kernel, out_shape=jax.ShapeDtypeStruct((32, 128), F32), in...]
where the time goes in v7:
time: 132 us; the launch traced here: 131 us
  Pallas kernels  129 us (98%)
  local copies, waits for them, and re-layouts  2.37 us (2%)
    pallas_call x1, Pallas kernels, body(): pl.pallas_call(kernel, out_shape=jax.ShapeDtypeStruct((32, 128), F32), in...  129 us

profile of v7, /device:TPU:1, one launch (start us, length us, event | category | flops | bytes accessed | tf_op | source)
XLA Modules:
  0.0 131.4 jit_solution(5149744303959820445)
XLA Ops:
  0.0 0.8 copy.3.start_ref
  0.8 0.0 copy-start
  0.8 0.9 copy-done
  1.8 129.0 %subspace.1 = f32[32,128]{1,0:T(8,128)S(1)} custom-call(bf16[16,8192]{1,0:T(8,128)(2,1)S(1)} %copy-done, f32[128,32]{1,0:T(8,128)S(1)} %copy.3.start_ref), custom_call_target="tpu_custom_call" | custom-call | tf_op jit(solution)/shard_map/subspace/pallas_call | solution.py:473
  130.8 0.6 copy.5
Async XLA Ops:
  0.8 1.0 copy-start

commit v8 on v7

--- a/solution.py
+++ b/solution.py
@@ -116,21 +116,18 @@
         return pl.ds(pl.multiple_of(t * 256 + h * 128, 128), 128)
 
     big, small = lax.div(z_lo, 2), lax.rem(z_lo, 2) * 4 + core * 2 + z_hi
-    halves = []
+    def half_wait(h):
+        sent = x_ref.at[:, pl.ds(0, 31 * 128)]
+        return (remote(sent, sent, z_send.at[h], z_recv.at[h], sibling),
+                remote(zbuf.at[h], zbuf.at[h], z_send.at[h], z_recv.at[h], sibling))
+
     for h in (0, 1):
         if h:
-            for copy in halves[0]:
-                copy.wait_send()
-        copies = []
+            half_wait(0)[0].wait_send()
         for o in far_first:
             t = lax.rem(me + o, 32)
-            copies.append(send(x_ref.at[:, columns(t, h)], zbuf.at[h, big, small],
-                               z_send.at[h, o], z_recv.at[h, o], line(t)))
-        halves.append(copies)
-    here = [pltpu.make_async_copy(x_ref.at[:, columns(me, h)], zbuf.at[h, big, small], local_sem.at[h])
-            for h in (0, 1)]
-    for copy in here:
-        copy.start()
+            send(x_ref.at[:, columns(t, h)], zbuf.at[h, big, small], z_send.at[h], z_recv.at[h], line(t))
+        pltpu.make_async_copy(x_ref.at[:, columns(me, h)], zbuf.at[h, big, small], z_recv.at[h]).start()
 
     giver = lax.div(row, 4) == y
     basis_slot = lax.rem(row, 4)
@@ -146,17 +143,15 @@
 
     @pl.when(giver)
     def _():
-        copy = pltpu.make_async_copy(start_ref, start.at[basis_slot], local_sem.at[2])
+        copy = pltpu.make_async_copy(start_ref, start.at[basis_slot], local_sem.at[0])
         copy.start()
         copy.wait()
 
     first = []
     for h in (0, 1):
-        here[h].wait()
-        for copy in halves[h]:
-            if h:
-                copy.wait_send()
-            copy.wait_recv()
+        half_wait(h)[1].wait_recv()
+        if h:
+            half_wait(1)[0].wait_send()
         pairs = []
         for k in (2, 1, 3):
             pairs.append((
@@ -359,21 +354,22 @@
             low = dot(jnp.concatenate(block[:2], axis=0), kern_lo[at], dims)
             return high[:32] + ((high[32:64] + low[:32]) + (high[64:] + low[32:]))
 
+        def product_wait(step, n):
+            three = income.at[step, n, pl.ds(0, 3)]
+            return remote(three, three, step_send.at[step, n], step_recv.at[step, n], sibling)
+
         def arrived(step, n):
-            for copy in copies[n]:
-                copy.wait()
+            product_wait(step, n).wait_recv()
             block = four(income.at[step, n])
             return dot(inverse, block, ((1,), (0,)), HIGH) if step in (3, 5) else block
 
         inverse = None
         gram_copies = None
-        copies = None
         for step in range(6):
             over_y = step % 2 == 0
             at = y if over_y else x
             scale_in, scale_out = (scale_col, scale_row) if over_y else (scale_row, scale_col)
             sums = None
-            sent = []
             for n in (0, 1):
                 if step:
                     basis[n] = arrived(step - 1, n)
@@ -384,9 +380,12 @@
                 for m in (0, 1):
                     income[step, m, at] = (sums[m] + term(over_y, 1, m, block)) * scale_out[m]
                     view = income.at[step, m, at]
-                    sent.append([send(view, view, step_send.at[step, m, k], step_recv.at[step, m, k],
-                                      along_y(k) if over_y else along_x(k)) for k in (2, 1, 3)])
-            copies = sent
+                    for k in (2, 1, 3):
+                        send(view, view, step_send.at[step, m], step_recv.at[step, m],
+                             along_y(k) if over_y else along_x(k))
+            if step:
+                for m in (0, 1):
+                    product_wait(step - 1, m).wait_send()
             if step in (2, 4):
                 n = step // 2 - 1
                 grams[n, y] = gram_of(jnp.concatenate(basis, axis=1))
@@ -436,6 +435,8 @@
                 def _():
                     last_rows[...] = last[:, i * 256:i * 256 + 128]
 
+        for m in (0, 1):
+            product_wait(5, m).wait_send()
         for copy in waits:
             copy.wait_send()
 
@@ -500,10 +501,10 @@
             pltpu.VMEM((32, 512), F32),
             pltpu.VMEM((32, 128), F32),
             pltpu.VMEM((4, 8, 128), F32),
-            DMA((3,)), DMA((2, 32)), DMA((2, 32)), DMA((2, 2, 4)), DMA((2, 2, 4)), DMA((2, 2, 4)), DMA((2, 2, 4)),
+            DMA((1,)), DMA((2,)), DMA((2,)), DMA((2, 2, 4)), DMA((2, 2, 4)), DMA((2, 2, 4)), DMA((2, 2, 4)),
             DMA((4,)), DMA((4,)), DMA((5,)), DMA((5,)), DMA((4,)), DMA((1,)), DMA((3,)), DMA((4,)),
             DMA((3,)), DMA((3,)), DMA((2,)), DMA((2,)), DMA((2, 4)), DMA((2, 2, 4)),
-            DMA((6, 2, 4)), DMA((6, 2, 4)), DMA((2, 4)), DMA((2, 4)), DMA((4, 4, 2)), DMA((4,)),
+            DMA((6, 2)), DMA((6, 2)), DMA((2, 4)), DMA((2, 4)), DMA((4, 4, 2)), DMA((4,)),
             DMA((4, 2, 2)), DMA((1,)),
         ],
         compiler_params=pltpu.CompilerParams(

time: 132 us -> 130 us (0.985)
  Pallas kernels: 129 us -> 127 us
    pallas_call x1, Pallas kernels: 129 us -> 127 us  [body(): pl.pallas_call(kernel, out_shape=jax.ShapeDtypeStruct((32, 128), F32), in...]
where the time goes in v8:
time: 130 us; the launch traced here: 129 us
  Pallas kernels  127 us (98%)
  local copies, waits for them, and re-layouts  2.37 us (2%)
    pallas_call x1, Pallas kernels, body(): pl.pallas_call(kernel, out_shape=jax.ShapeDtypeStruct((32, 128), F32), in...  127 us

profile of v8, /device:TPU:1, one launch (start us, length us, event | category | flops | bytes accessed | tf_op | source)
XLA Modules:
  0.0 129.4 jit_solution(14082195364728273905)
XLA Ops:
  0.0 0.8 copy.3.start_ref
  0.8 0.0 copy-start
  0.8 0.9 copy-done
  1.8 127.0 %subspace.1 = f32[32,128]{1,0:T(8,128)S(1)} custom-call(bf16[16,8192]{1,0:T(8,128)(2,1)S(1)} %copy-done, f32[128,32]{1,0:T(8,128)S(1)} %copy.3.start_ref), custom_call_target="tpu_custom_call" | custom-call | tf_op jit(solution)/shard_map/subspace/pallas_call | solution.py:474
  128.7 0.6 copy.5
Async XLA Ops:
  0.8 1.0 copy-start

commit v9 on v8

--- a/solution.py
+++ b/solution.py
@@ -147,39 +147,36 @@
         copy.start()
         copy.wait()
 
-    first = []
+    def three(ref, h, sems, n):
+        view = ref.at[h, pl.ds(0, 3)]
+        return remote(view, view, sems[0].at[h, n], sems[1].at[h, n], sibling)
+
+    plane, gathered = (plane_send, plane_recv), (gather_send, gather_recv)
     for h in (0, 1):
         half_wait(h)[1].wait_recv()
-        if h:
-            half_wait(1)[0].wait_send()
-        pairs = []
         for k in (2, 1, 3):
-            pairs.append((
-                send(zbuf.at[h, lax.rem(x + k, 4)], abuf.at[h, y, :, x],
-                     plane_send.at[h, 0, k], plane_recv.at[h, 0, k], along_x(k)),
-                send(zbuf.at[h, lax.rem(y + k, 4)], bbuf.at[h, y, :, x],
-                     plane_send.at[h, 1, k], plane_recv.at[h, 1, k], along_y(k))))
-        first.append(pairs)
+            send(zbuf.at[h, lax.rem(x + k, 4)], abuf.at[h, y, :, x],
+                 plane_send.at[h, 0], plane_recv.at[h, 0], along_x(k))
+            send(zbuf.at[h, lax.rem(y + k, 4)], bbuf.at[h, y, :, x],
+                 plane_send.at[h, 1], plane_recv.at[h, 1], along_y(k))
         abuf[h, y, :, x] = zbuf[h, x]
         bbuf[h, y, :, x] = zbuf[h, y]
-    gathers = []
+    half_wait(1)[0].wait_send()
     for h in (0, 1):
-        group_copies = []
-        for copy, _ in first[h]:
-            copy.wait()
+        three(zbuf, h, plane, 0).wait_recv()
         for k in (2, 1, 3):
-            group_copies.append(send_pieces(4, abuf.at[h, y], abuf.at[h, y],
-                                     gather_send.at[h, 0, k], gather_recv.at[h, 0, k], along_y(k)))
-        for _, copy in first[h]:
-            copy.wait()
+            send_pieces(4, abuf.at[h, y], abuf.at[h, y], gather_send.at[h, 0], gather_recv.at[h, 0], along_y(k))
+        three(zbuf, h, plane, 1).wait_recv()
         for k in (2, 1, 3):
-            group_copies.append(send_pieces(4, bbuf.at[h, :, :, x], bbuf.at[h, :, :, x],
-                                     gather_send.at[h, 1, k], gather_recv.at[h, 1, k], along_x(k)))
-        gathers.append(group_copies)
-
+            send_pieces(4, bbuf.at[h, :, :, x], bbuf.at[h, :, :, x],
+                        gather_send.at[h, 1], gather_recv.at[h, 1], along_x(k))
     for h in (0, 1):
-        for copy in gathers[h]:
-            copy.wait()
+        for n in (0, 1):
+            three(zbuf, h, plane, n).wait_send()
+
+    for h in (0, 1):
+        three(abuf, h, gathered, 0).wait()
+        three(bbuf, h, gathered, 1).wait()
         b = jnp.concatenate([bbuf[h, q].reshape(512, 128) for q in range(4)], axis=1)
         b_wide = b.astype(F32)
         ones = jnp.ones((16, 512), BF16)
@@ -292,14 +289,14 @@
                 send_pieces(4, ref.at[my_half, :], ref.at[my_half, :], core_send.at[n], core_recv.at[n], sibling)
 
         ones = jnp.ones((16, 512), BF16)
-        deg_row[core, y] = (dot(ones, half_hi, ((1,), (1,))) + dot(ones, half_lo, ((1,), (1,))))[:8]
-        deg_col[core, x] = (dot(ones[:, :256], half_hi, ((1,), (0,)))
+        deg_row[core * 4 + y] = (dot(ones, half_hi, ((1,), (1,))) + dot(ones, half_lo, ((1,), (1,))))[:8]
+        deg_col[core * 4 + x] = (dot(ones[:, :256], half_hi, ((1,), (0,)))
                             + dot(ones[:, :256], half_lo, ((1,), (0,))))[:8]
 
         def degree_copies(k):
-            row_view, col_view = deg_row.at[core, y], deg_col.at[core, x]
-            return (remote(row_view, row_view, deg_send.at[0, k], deg_recv.at[0, core, k], along_y(k, 0)),
-                    remote(col_view, col_view, deg_send.at[1, k], deg_recv.at[1, core, k], along_x(k, 0)))
+            row_view, col_view = deg_row.at[core * 4 + y], deg_col.at[core * 4 + x]
+            return (remote(row_view, row_view, deg_send.at[0], deg_recv.at[0], along_y(k, 0)),
+                    remote(col_view, col_view, deg_send.at[1], deg_recv.at[1], along_x(k, 0)))
 
         @pl.when(core == 1)
         def _():
@@ -308,19 +305,15 @@
                     copy.start()
             for copy in swaps:
                 copy.wait_send()
-            for k in range(4):
-                for copy in degree_copies(k):
-                    copy.wait_send()
+            for n, ref in enumerate((deg_row, deg_col)):
+                view = ref.at[pl.ds(0, 4)]
+                remote(view, view, deg_send.at[n], deg_recv.at[n], sibling).wait_send()
 
     @pl.when(iterates & (core == 0))
     def _():
-        def degree_copy(n, c, k):
-            ref = (deg_row, deg_col)[n].at[c, 0]
-            return remote(ref, ref, deg_send.at[n, k], deg_recv.at[n, c, k], sibling)
-
         for k in (2, 1, 3):
-            for n, ref, target in ((0, deg_row.at[0, y], along_y(k)), (1, deg_col.at[0, x], along_x(k))):
-                remote(ref, ref, deg_send.at[n, k], deg_recv.at[n, 0, k], target).start()
+            for n, ref, target in ((0, deg_row.at[y], along_y(k)), (1, deg_col.at[x], along_x(k))):
+                send(ref, ref, deg_send.at[n], deg_recv.at[n], target)
         wide[...] = jnp.zeros_like(wide)
 
         def gram_of(block):
@@ -336,14 +329,14 @@
         other_half = pl.ds(256, 256)
         for n, ref in enumerate((kern_hi, kern_lo)):
             remote(ref.at[other_half, :], ref.at[other_half, :], core_send.at[n], core_recv.at[n], sibling).wait_recv()
-        for n in (0, 1):
-            for k in (1, 2, 3):
-                degree_copy(n, 0, k).wait()
-            for k in range(4):
-                degree_copy(n, 1, k).wait_recv()
-        row_sums = jnp.concatenate([four(deg_row.at[0]), four(deg_row.at[1])], axis=1)[0:1]
+        for n, ref in enumerate((deg_row, deg_col)):
+            sent, arriving = ref.at[pl.ds(0, 3)], ref.at[pl.ds(0, 7)]
+            remote(arriving, arriving, deg_send.at[n], deg_recv.at[n], sibling).wait_recv()
+            remote(sent, sent, deg_send.at[n], deg_recv.at[n], sibling).wait_send()
+        low_half, high_half = pl.ds(0, 4), pl.ds(4, 4)
+        row_sums = jnp.concatenate([four(deg_row.at[low_half]), four(deg_row.at[high_half])], axis=1)[0:1]
         scale_row = 1.0 / jnp.sqrt(row_sums)
-        scale_col = 1.0 / jnp.sqrt((four(deg_col.at[0]) + four(deg_col.at[1]))[0:1])
+        scale_col = 1.0 / jnp.sqrt((four(deg_col.at[low_half]) + four(deg_col.at[high_half]))[0:1])
         scale_row = scale_row[:, :256], scale_row[:, 256:]
         scale_col = scale_col[:, :256], scale_col[:, 256:]
 
@@ -493,17 +486,17 @@
             pltpu.VMEM((384, 640), F32),
             pltpu.VMEM((512, 512), BF16),
             pltpu.VMEM((512, 512), BF16),
-            pltpu.VMEM((2, 4, 8, 256), F32),
-            pltpu.VMEM((2, 4, 8, 512), F32),
+            pltpu.VMEM((8, 8, 256), F32),
+            pltpu.VMEM((8, 8, 512), F32),
             pltpu.VMEM((128, 512), F32),
             pltpu.VMEM((6, 2, 4, 32, 256), F32),
             pltpu.VMEM((2, 4, 32, 128), F32),
             pltpu.VMEM((32, 512), F32),
             pltpu.VMEM((32, 128), F32),
             pltpu.VMEM((4, 8, 128), F32),
-            DMA((1,)), DMA((2,)), DMA((2,)), DMA((2, 2, 4)), DMA((2, 2, 4)), DMA((2, 2, 4)), DMA((2, 2, 4)),
+            DMA((1,)), DMA((2,)), DMA((2,)), DMA((2, 2)), DMA((2, 2)), DMA((2, 2)), DMA((2, 2)),
             DMA((4,)), DMA((4,)), DMA((5,)), DMA((5,)), DMA((4,)), DMA((1,)), DMA((3,)), DMA((4,)),
-            DMA((3,)), DMA((3,)), DMA((2,)), DMA((2,)), DMA((2, 4)), DMA((2, 2, 4)),
+            DMA((3,)), DMA((3,)), DMA((2,)), DMA((2,)), DMA((2,)), DMA((2,)),
             DMA((6, 2)), DMA((6, 2)), DMA((2, 4)), DMA((2, 4)), DMA((4, 4, 2)), DMA((4,)),
             DMA((4, 2, 2)), DMA((1,)),
         ],

time: 130 us -> 129 us (level)
  no operation moved by 1% of the time
where the time goes in v9:
time: 129 us
  Pallas kernels  126 us (98%)
  local copies, waits for them, and re-layouts  2.37 us (2%)
    pallas_call x1, Pallas kernels, body(): pl.pallas_call(kernel, out_shape=jax.ShapeDtypeStruct((32, 128), F32), in...  126 us

profile of v9, /device:TPU:1, one launch (start us, length us, event | category | flops | bytes accessed | tf_op | source)
XLA Modules:
  0.0 128.7 jit_solution(11981199189710699133)
XLA Ops:
  0.0 0.8 copy.3.start_ref
  0.8 0.0 copy-start
  0.8 0.9 copy-done
  1.8 126.4 %subspace.1 = f32[32,128]{1,0:T(8,128)S(1)} custom-call(bf16[16,8192]{1,0:T(8,128)(2,1)S(1)} %copy-done, f32[128,32]{1,0:T(8,128)S(1)} %copy.3.start_ref), custom_call_target="tpu_custom_call" | custom-call | tf_op jit(solution)/shard_map/subspace/pallas_call | solution.py:467
  128.1 0.6 copy.5
Async XLA Ops:
  0.8 1.0 copy-start

commit v10 on v9

--- a/solution.py
+++ b/solution.py
@@ -263,13 +263,16 @@
         first_row = jnp.where(2 * x + core == 0, 128, 0)
         first_lane = jnp.where(y == 0, 128, 0)
         run = jnp.where((rows >= first_row) & (lanes >= first_lane), ext[...], 0.0)
+        run = jnp.concatenate(
+            [pltpu.roll(run[r:r + 8], (640 - r) % 640, 1) for r in range(0, 384, 8)], axis=0)
         stride = LAGS // 2
+        while stride >= 8:
+            run = run[stride:] + run[:-stride]
+            stride //= 2
+        run = jnp.concatenate(
+            [pltpu.roll(run[r:r + 8], r + 120, 1) for r in range(0, 264, 8)], axis=0)
         while stride >= 1:
-            turned = pltpu.roll(run, stride, 1)
-            if stride >= 8:
-                run = run[stride:] + turned[:-stride]
-            else:
-                run = run + pltpu.roll(turned, stride, 0)
+            run = run + pltpu.roll(pltpu.roll(run, stride, 1), stride, 0)
             stride //= 2
         lagged = run[8:, 128:]
         i = lax.broadcasted_iota(jnp.int32, (256, 512), 0) + (x * 512 + core * 256)

time: 129 us -> 129 us (level)
  no operation moved by 1% of the time
where the time goes in v10:
time: 129 us; the launch traced here: 128 us
  Pallas kernels  126 us (98%)
  local copies, waits for them, and re-layouts  2.37 us (2%)
    pallas_call x1, Pallas kernels, body(): pl.pallas_call(kernel, out_shape=jax.ShapeDtypeStruct((32, 128), F32), in...  126 us

profile of v10, /device:TPU:1, one launch (start us, length us, event | category | flops | bytes accessed | tf_op | source)
XLA Modules:
  0.0 128.3 jit_solution(17364341517557282952)
XLA Ops:
  0.0 0.8 copy.3.start_ref
  0.8 0.0 copy-start
  0.8 0.9 copy-done
  1.8 126.0 %subspace.1 = f32[32,128]{1,0:T(8,128)S(1)} custom-call(bf16[16,8192]{1,0:T(8,128)(2,1)S(1)} %copy-done, f32[128,32]{1,0:T(8,128)S(1)} %copy.3.start_ref), custom_call_target="tpu_custom_call" | custom-call | tf_op jit(solution)/shard_map/subspace/pallas_call | solution.py:470
  127.7 0.6 copy.5
Async XLA Ops:
  0.8 1.0 copy-start

commit v11 on v10

--- a/solution.py
+++ b/solution.py
@@ -205,15 +205,15 @@
         send(own.at[lax.rem(z + d, 16)], rs_up.at[d - 5], rs_send.at[0], rs_recv.at[0], at_plane(d - 4))
         if d < 8:
             send(own.at[lax.rem(z + 16 - d, 16)], rs_down.at[d - 5], rs_send.at[1], rs_recv.at[1], at_plane(4 - d))
-    for d in (3, 2, 1):
-        send(own.at[lax.rem(z + d, 16)], rs_near.at[d - 1], rs_send.at[2], rs_recv.at[2], at_plane(d))
-        send(own.at[lax.rem(z + 16 - d, 16)], rs_near.at[d + 2], rs_send.at[2], rs_recv.at[2], at_plane(-d))
     remote(rs_up, rs_up, rs_send.at[0], rs_recv.at[0], sibling).wait_recv()
     rs_sum[0] = own[lax.rem(z + 4, 16)] + four(rs_up)
     last_up = send(rs_sum.at[0], rs_last.at[0], rs_send.at[3], rs_recv.at[3], at_plane(4))
     remote(rs_down, rs_down, rs_send.at[1], rs_recv.at[1], sibling).wait_recv()
     rs_sum[1] = own[lax.rem(z + 12, 16)] + (rs_down[0] + rs_down[1] + rs_down[2])
     last_down = send(rs_sum.at[1], rs_last.at[1], rs_send.at[4], rs_recv.at[4], at_plane(-4))
+    for d in (3, 2, 1):
+        send(own.at[lax.rem(z + d, 16)], rs_near.at[d - 1], rs_send.at[2], rs_recv.at[2], at_plane(d))
+        send(own.at[lax.rem(z + 16 - d, 16)], rs_near.at[d + 2], rs_send.at[2], rs_recv.at[2], at_plane(-d))
     remote(rs_near, rs_near, rs_send.at[2], rs_recv.at[2], sibling).wait()
     near = own[z] + ((rs_near[0] + rs_near[1]) + (rs_near[2] + rs_near[3]) + (rs_near[4] + rs_near[5]))
     last_up.wait()

time: 129 us -> 130 us (level)
  Pallas kernels: 126 us -> 128 us
    pallas_call x1, Pallas kernels: 126 us -> 128 us  [body(): pl.pallas_call(kernel, out_shape=jax.ShapeDtypeStruct((32, 128), F32), in...]
where the time goes in v11:
time: 130 us
  Pallas kernels  128 us (98%)
  local copies, waits for them, and re-layouts  2.37 us (2%)
    pallas_call x1, Pallas kernels, body(): pl.pallas_call(kernel, out_shape=jax.ShapeDtypeStruct((32, 128), F32), in...  128 us

profile of v11, /device:TPU:1, one launch (start us, length us, event | category | flops | bytes accessed | tf_op | source)
XLA Modules:
  0.0 129.9 jit_solution(6588223182809710026)
XLA Ops:
  0.0 0.8 copy.3.start_ref
  0.8 0.0 copy-start
  0.8 0.9 copy-done
  1.8 127.5 %subspace.1 = f32[32,128]{1,0:T(8,128)S(1)} custom-call(bf16[16,8192]{1,0:T(8,128)(2,1)S(1)} %copy-done, f32[128,32]{1,0:T(8,128)S(1)} %copy.3.start_ref), custom_call_target="tpu_custom_call" | custom-call | tf_op jit(solution)/shard_map/subspace/pallas_call | solution.py:470
  129.3 0.6 copy.5
Async XLA Ops:
  0.8 1.0 copy-start
